TPU v7x, 256 devices: a whole 4x4x8 slice. The times are simulated.
256 devices in a mesh: band: 32 (over x, z), chan: 8 (over y, core).
Axes of the slice: x: 4, y: 4, z: 8, core: 2. Of those that a mesh axis runs over, the one named last changes fastest.
Arguments:
- node_values: bfloat16 [1, 224, 131072], P(None, 'chan', 'band'), may hold values from -6 to 6
- block_slot: int32 [1024], P('band'), may hold values from 0 to 63, as said below
- cell_ref: int32 [3, 256, 1440], P(None, 'band'), may hold values from 0 to 8191, as said below
- cell_weight: float32 [3, 256, 1440], P(None, 'band'), may hold values from 0.2 to 1
- target_spectrum: bfloat16 [1, 224, 256, 2, 640], P(None, 'chan', 'band'), may hold values from -48 to 48
- spec_weight: float32 [640], replicated, may hold values from 0.1 to 1
Outputs:
- node_grad: bfloat16 [1, 224, 131072], P(None, 'chan', 'band')
Inputs may be any that keep to these rules, and one draw needn't show every extreme that they name: `block_slot`: each node owner's 32 consecutive entries are distinct slots; slot v belongs to band owner v // 2, and a node owner fills either none or all 2 slots of a band owner. Some band owner gets 2 blocks from every node owner, and every band owner gets blocks from at least one node owner. `cell_ref`: an entry of latitude row a always names a slot e of step one that its node owner fills with a block for band owner a // 8.
All inputs are finite; a program needn't handle non-finite values.
Results may differ from a plain program's by a relative error of at most 0.0056.
Values may be sent and summed in bfloat16 or wider, within the bound.
No kernel may reach another device: no remote copies, remote signals or barrier semaphores. Data moves between devices by JAX's collectives and lax.ppermute only.
A program may use at most 128 MiB of HBM per device.

v0:
```python
import math

import jax
import jax.numpy as jnp
from jax import lax
from jax.sharding import PartitionSpec as P

C = 224
LON = 1440
K = 640
J = 3
NB = 128
LAT_DEV = 8
NBLK_DEV = 32


epsilon = 1e-06


def dft_table():
    wavenumber = jnp.arange(K, dtype=jnp.int32)[:, None]
    column = jnp.arange(LON, dtype=jnp.int32)[None, :]
    phase_count = wavenumber * column % LON
    phase_angle = 2.0 * math.pi / LON * phase_count.astype(jnp.float32)
    norm_factor = 1.0 / math.sqrt(LON)
    return jnp.stack(
        [jnp.cos(phase_angle) * norm_factor, -jnp.sin(phase_angle) * norm_factor]
    ).astype(jnp.bfloat16)


def lat_weights(first_row, row_count, lat_total):
    row_index = first_row + jnp.arange(row_count, dtype=jnp.int32)
    latitude = (row_index.astype(jnp.float32) + 0.5) * (math.pi / lat_total) - 0.5 * math.pi
    return jnp.cos(latitude)


def power_sums(spectrum, target, lat_weight):
    predicted = spectrum.astype(jnp.float32)
    observed = target.astype(jnp.float32)
    weight = lat_weight[None, :, None, None]
    return (
        jnp.sum(weight * predicted * predicted, axis=(1, 2)),
        jnp.sum(weight * observed * observed, axis=(1, 2)),
        jnp.sum(weight * predicted * observed, axis=(1, 2)),
    )


def amplitude_grad(spectrum, target, lat_weight, pred_power, true_power, cross_sum, loss_scale):
    amp_pred = jnp.sqrt(pred_power + epsilon)
    amp_true = jnp.sqrt(true_power + epsilon)
    d_pred = (
        loss_scale
        * (
            4.0 * amp_pred
            - 2.0 * amp_true
            - cross_sum * (1.0 / amp_true - amp_true / (amp_pred * amp_pred))
        )
        / (2.0 * amp_pred)
    )
    d_cross = -loss_scale * (amp_pred / amp_true + amp_true / amp_pred)
    weight = lat_weight[None, :, None, None]
    result = weight * (
        2.0 * spectrum.astype(jnp.float32) * d_pred[:, None, None, :]
        + target.astype(jnp.float32) * d_cross[:, None, None, :]
    )
    return result.astype(jnp.bfloat16)


def shards(node_values, block_slot, cell_ref, cell_weight, target_spectrum, spec_weight):
    band_count = lax.axis_size("band")
    band_index = lax.axis_index("band")
    samples, chan_local, nodes_local = node_values.shape
    item_count = samples * chan_local
    capacity = max(2, 2 * NBLK_DEV // band_count)
    slot_count = band_count * capacity
    blocks = node_values.reshape(item_count, NBLK_DEV, NB)
    outgoing = (
        jnp.zeros((item_count, slot_count, NB), jnp.bfloat16).at[:, block_slot, :].set(blocks)
    )
    received = lax.all_to_all(outgoing, "band", split_axis=1, concat_axis=1, tiled=True)
    flattened = received.reshape(received.shape[0], slot_count * NB)
    grid_values = jnp.zeros((received.shape[0], LAT_DEV, LON), jnp.float32)
    for regrid_member in range(J):
        grid_values = (
            grid_values + cell_weight[regrid_member][None] * flattened[:, cell_ref[regrid_member]]
        )
    grid_values = grid_values.astype(jnp.bfloat16)
    transform = dft_table()
    spectrum = jnp.einsum(
        "pal,rkl->park", grid_values, transform, preferred_element_type=jnp.float32
    ).astype(jnp.bfloat16)
    target = target_spectrum.reshape(item_count, LAT_DEV, 2, K)
    lat_total = LAT_DEV * band_count
    local_weight = lat_weights(band_index * LAT_DEV, LAT_DEV, lat_total)
    observed = target.astype(jnp.float32)
    local_true = jnp.sum(local_weight[None, :, None, None] * observed * observed, axis=(1, 2))
    energy_part = jnp.sum(
        (local_true * spec_weight[None, :]).reshape(samples, chan_local, K), axis=(1, 2)
    )
    energy = lax.psum(energy_part, ("band", "chan")) / (C * K * lat_total) + epsilon
    row_energy = jnp.repeat(energy, chan_local)
    moved_pred, moved_true = (
        lax.all_to_all(spectrum, "band", split_axis=3, concat_axis=1, tiled=True),
        lax.all_to_all(target, "band", split_axis=3, concat_axis=1, tiled=True),
    )
    block_width = moved_pred.shape[3]
    full_weight = lat_weights(0, lat_total, lat_total)
    pred_power, true_power, cross_sum = power_sums(moved_pred, moved_true, full_weight)
    block_weight = lax.dynamic_slice_in_dim(spec_weight, band_index * block_width, block_width)
    loss_scale = block_weight[None, :] / row_energy[:, None]
    moved_grad = amplitude_grad(
        moved_pred, moved_true, full_weight, pred_power, true_power, cross_sum, loss_scale
    )
    spectrum_grad = lax.all_to_all(moved_grad, "band", split_axis=1, concat_axis=3, tiled=True)
    grid_grad = jnp.einsum(
        "park,rkl->pal", spectrum_grad, transform, preferred_element_type=jnp.float32
    )
    buffer_grad = jnp.zeros((item_count, slot_count * NB), jnp.float32)
    for member in range(J):
        buffer_grad = buffer_grad.at[:, cell_ref[member]].add(cell_weight[member][None] * grid_grad)
    buffer_grad = buffer_grad.astype(jnp.bfloat16).reshape(item_count, slot_count, NB)
    returned = lax.all_to_all(buffer_grad, "band", split_axis=1, concat_axis=1, tiled=True)
    node_grad = returned[:, block_slot, :]
    return node_grad.reshape(samples, chan_local, nodes_local)


def solution(mesh):
    in_specs = (
        P(None, "chan", "band"),
        P("band"),
        P(None, "band", None),
        P(None, "band", None),
        P(None, "chan", "band", None, None),
        P(),
    )
    out_specs = P(None, "chan", "band")
    return jax.shard_map(shards, mesh=mesh, in_specs=in_specs, out_specs=out_specs, check_vma=False)
```

profile of v0, /device:TPU:32, one launch (start us, length us, event | category | flops | bytes accessed | tf_op | source)
XLA Modules:
  0.0 623.3 jit_solution(9360717831462960317)
XLA Ops:
  2.7 3.8 scatter_fusion
  6.6 11.3 %all-to-all-start = ((bf16[28,64,128]{2,0,1:T(8,128)(2,1)}), bf16[28,64,128]{2,0,1:T(8,128)(2,1)}, u32[]{:S(2)}, u32[]{:S(2)}) async-start(bf16[28,64,128]{2,0,1:T(8,128)(2,1)} %scatter_fusion), calls=%async_computation | async-start | bytes 1048576 | tf_op jit(solution)/shard_map/all_to_all | solution.py:80
  18.1 4.0 copy.133
  22.1 2.2 bitcast_bitcast_fusion
  24.4 6.7 %reshape.358 = bf16[32,2,4480]{2,1,0:T(2,128)(2,1)} reshape(bf16[640,2,8,28]{3,2,1,0:T(8,128)(2,1)S(1)} %bitcast_bitcast_fusion) | data formatting | bytes 1146880
  31.2 4.3 all-to-all-done
  35.5 5.9 all-to-all-start.2
  41.4 17.0 %multiply_convert_fusion = (bf16[1,640,1440]{1,2,0:T(8,128)(2,1)}, bf16[1,640,1440]{1,2,0:T(8,128)(2,1)}) fusion(), kind=kLoop, calls=%fused_computation.23 | loop fusion | flops 12902400 | bytes 3686400 | tf_op jit(solution)/shard_map/convert.11
  58.4 2.0 copy.137
  60.4 23.8 %gather_fusion = bf16[11520,28]{1,0:T(8,128)(2,1)} fusion(bf16[28,8192]{0,1:T(8,128)(2,1)S(1)} %bitcast.114, s32[12288]{0:T(1024)S(1)} %pad_clamp_fusion.2), kind=kCustom, calls=%fused_computation | custom fusion | bytes 1336320 | tf_op jit(solution)/shard_map/gather | solution.py:85
  84.2 4.2 copy.107
  88.4 23.8 %gather_fusion.1 = bf16[11520,28]{1,0:T(8,128)(2,1)} fusion(bf16[28,8192]{0,1:T(8,128)(2,1)S(1)} %bitcast.115, s32[12288]{0:T(1024)S(1)} %pad_clamp_fusion.1), kind=kCustom, calls=%fused_computation.1 | custom fusion | bytes 1336320 | tf_op jit(solution)/shard_map/gather | solution.py:85
  112.2 4.3 copy.109
  116.5 23.8 %gather_fusion.2 = bf16[11520,28]{1,0:T(8,128)(2,1)} fusion(bf16[28,8192]{0,1:T(8,128)(2,1)S(1)} %bitcast.116, s32[12288]{0:T(1024)S(1)} %pad_clamp_fusion), kind=kCustom, calls=%fused_computation.2 | custom fusion | bytes 1336320 | tf_op jit(solution)/shard_map/gather | solution.py:85
  140.3 4.4 copy.111
  144.7 4.7 fusion.14
  149.4 4.6 copy.112
  154.0 6.7 %reshape.360 = bf16[32,2,4480]{2,1,0:T(2,128)(2,1)} reshape(bf16[640,2,8,28]{3,2,1,0:T(8,128)(2,1)S(1)} %bitcast.119) | data formatting | bytes 1146880
  160.8 9.8 %all-to-all-start.1 = ((bf16[32,2,4480]{2,1,0:T(2,128)(2,1)}), bf16[32,2,4480]{2,1,0:T(2,128)(2,1)}, u32[]{:S(2)}, u32[]{:S(2)}) async-start(bf16[32,2,4480]{2,1,0:T(2,128)(2,1)} %reshape.360), calls=%async_computation.1 | async-start | bytes 1146880 | tf_op jit(solution)/shard_map/all_to_all | solution.py:103
  172.1 76.8 %psum.7 = f32[1]{0:T(128)} all-reduce(f32[1]{0:T(128)} %bitcast.17), channel_id=1, replica_groups=mesh['band'=32,'chan'=8] {'band','chan'}, use_global_device_ids=true, to_apply=%region_3.4 | all-reduce | flops 1 | bytes 8 | tf_op jit(solution)/shard_map/psum | solution.py:100
  249.6 8.1 %reshape.359 = bf16[640,2,8,28]{3,2,1,0:T(8,128)(2,1)S(1)} reshape(bf16[32,2,4480]{2,1,0:T(2,128)(2,1)} %all-to-all-done.2) | data formatting | bytes 1146880
  257.7 3.7 copy.119
  261.4 9.7 %reshape.275 = f32[28,8,2,32,20]{4,3,1,2,0:T(8,128)} reshape(bf16[28,8,2,640]{3,1,2,0:T(8,128)(2,1)S(1)} %copy.119) | data formatting | bytes 1720320 | tf_op jit(solution)/shard_map/convert_element_type | solution.py:39
  271.1 9.2 %copy.122 = f32[28,32,8,2,20]{0,2,1,4,3:T(8,128)} copy(f32[28,32,8,2,20]{4,1,2,3,0:T(8,128)} %bitcast.117) | data formatting | bytes 2293760 | tf_op jit(solution)/shard_map/convert_element_type | solution.py:39
  280.3 8.1 %reshape.361 = bf16[640,2,8,28]{3,2,1,0:T(8,128)(2,1)S(1)} reshape(bf16[32,2,4480]{2,1,0:T(2,128)(2,1)} %all-to-all-done.1) | data formatting | bytes 1146880
  288.4 3.7 copy.113
  292.1 9.9 %reshape.276 = f32[28,8,2,32,20]{4,3,1,2,0:T(8,128)} reshape(bf16[28,8,2,640]{3,1,2,0:T(8,128)(2,1)S(1)} %copy.113) | data formatting | bytes 1720320 | tf_op jit(solution)/shard_map/convert_element_type | solution.py:63
  302.0 7.0 %fusion.1 = (f32[28,20]{1,0:T(8,128)S(1)}, f32[28,20]{1,0:T(8,128)S(1)}, f32[28,20]{1,0:T(8,128)S(1)}) fusion(f32[32,8]{0,1:T(8,128)S(1)} %add_cosine_fusion, f32[28,8,2,32,20]{4,3,1,2,0:T(8,128)} %reshape.275, f32[28,8,2,32,20]{4,3,1,2,0:T(8,128)} %reshape.276), kind=kLoop, calls=%fused_computation.12 | loop fusion | flops 2292080 | bytes 2301504 | tf_op jit(solution)/shard_map/reduce_sum | solution.py:44
  309.2 9.2 %copy.114 = f32[28,32,8,2,20]{0,2,1,4,3:T(8,128)} copy(f32[28,32,8,2,20]{4,1,2,3,0:T(8,128)} %bitcast.118) | data formatting | bytes 2293760 | tf_op jit(solution)/shard_map/convert_element_type | solution.py:63
  318.5 5.5 fusion.5
  324.0 2.7 copy.147
  326.7 6.0 reshape.362
  332.7 26.4 %all_to_all.46 = bf16[32,2,4480]{2,1,0:T(2,128)(2,1)} all-to-all(bf16[32,2,4480]{2,1,0:T(2,128)(2,1)S(1)} %reshape.362), channel_id=1, replica_groups=mesh['band'=32,'chan'=8] {'band'}, dimensions={0} | all-to-all | bytes 1146880 | tf_op jit(solution)/shard_map/all_to_all | solution.py:114
  359.1 9.8 %reshape.363 = bf16[256,20,2,28]{3,2,1,0:T(2,128)(2,1)S(1)} reshape(bf16[32,2,4480]{2,1,0:T(2,128)(2,1)} %all_to_all.46) | data formatting | bytes 1146880
  368.9 2.1 copy.145
  371.1 9.9 %copy.125 = bf16[28,8,2,32,20]{4,3,1,2,0:T(8,128)(2,1)} copy(bf16[28,8,2,32,20]{0,1,3,4,2:T(8,128)(2,1)} %bitcast.124) | data formatting | bytes 1146880 | tf_op jit(solution)/shard_map/all_to_all | solution.py:114
  380.9 8.2 %all_to_all.39 = bf16[28,8,2,640]{3,1,2,0:T(8,128)(2,1)} reshape(bf16[28,8,2,32,20]{4,3,1,2,0:T(8,128)(2,1)} %copy.125) | data formatting | bytes 1146880 | tf_op jit(solution)/shard_map/all_to_all | solution.py:114
  389.2 4.6 multiply_bitcast_fusion
  393.8 5.0 copy.134
  398.8 3.9 copy.135
  402.7 3.9 copy.136
  406.7 65.9 %scatter_custom_fusion.1 = f32[28,8192]{0,1:T(8,128)} fusion(s32[11520]{0:T(1024)S(1)} %reshape.320, f32[11520,28]{1,0:T(8,128)} %bitcast.128, f32[]{:T(128)} %constant.22.clone.1), kind=kCustom, calls=%fused_computation.32 | custom fusion | flops 322560 | bytes 918016 | tf_op jit(solution)/shard_map/scatter-add | solution.py:120
  472.6 61.4 %scatter_fusion.1 = f32[28,8192]{0,1:T(8,128)} fusion(f32[28,8192]{0,1:T(8,128)} %scatter_custom_fusion.1, s32[11520]{0:T(1024)S(1)} %reshape.288, f32[11520,28]{1,0:T(8,128)} %bitcast.126), kind=kCustom, calls=%fused_computation.6 | custom fusion | flops 322560 | bytes 3916800 | tf_op jit(solution)/shard_map/scatter-add | solution.py:120
  534.0 61.4 %scatter_fusion.2 = f32[28,8192]{0,1:T(8,128)} fusion(f32[28,8192]{0,1:T(8,128)} %scatter_fusion.1, s32[11520]{0:T(1024)S(1)} %reshape.296, f32[11520,28]{1,0:T(8,128)} %bitcast.125), kind=kCustom, calls=%fused_computation.7 | custom fusion | flops 322560 | bytes 3916800 | tf_op jit(solution)/shard_map/scatter-add | solution.py:120
  595.5 2.4 convert_element_type.119
  597.9 1.7 copy.129
  599.5 4.8 all-to-all-start.4
  604.4 16.9 %all-to-all-done.4 = bf16[28,64,128]{2,0,1:T(8,128)(2,1)S(1)} async-done(((bf16[28,64,128]{2,0,1:T(8,128)(2,1)}), bf16[28,64,128]{2,0,1:T(8,128)(2,1)S(1)}, u32[]{:S(2)}, u32[]{:S(2)}) %all-to-all-start.4) | async-done | bytes 458784 | tf_op jit(solution)/shard_map/all_to_all | solution.py:122
  (56 shorter events, 6.6 us)
Async XLA Ops:
  0.0 17.8 %copy-start.4 = (s32[3,8,1440]{2,1,0:T(8,128)S(1)}, s32[3,8,1440]{2,1,0:T(8,128)}, u32[]{:S(2)}) copy-start(s32[3,8,1440]{2,1,0:T(8,128)} %param.8) | copy-start | bytes 414724
  0.0 18.1 %copy-start = (bf16[1,28,8,2,640]{4,3,2,1,0:T(2,128)(2,1)S(1)}, bf16[1,28,8,2,640]{4,3,2,1,0:T(2,128)(2,1)}, u32[]{:S(2)}) copy-start(bf16[1,28,8,2,640]{4,3,2,1,0:T(2,128)(2,1)} %param.10) | copy-start | bytes 1720324
  6.6 28.9 %all-to-all-start = ((bf16[28,64,128]{2,0,1:T(8,128)(2,1)}), bf16[28,64,128]{2,0,1:T(8,128)(2,1)}, u32[]{:S(2)}, u32[]{:S(2)}) async-start(bf16[28,64,128]{2,0,1:T(8,128)(2,1)} %scatter_fusion), calls=%async_computation | async-start | bytes 1048576 | tf_op jit(solution)/shard_map/all_to_all | solution.py:80
  22.1 9.0 %copy-start.5 = (f32[3,8,1440]{2,1,0:T(8,128)S(1)}, f32[3,8,1440]{2,1,0:T(8,128)}, u32[]{:S(2)}) copy-start(f32[3,8,1440]{2,1,0:T(8,128)} %param.9) | copy-start | bytes 414724
  31.1 113.6 %copy-start.6 = (f32[8,1440]{1,0:T(8,128)}, f32[8,1440]{1,0:T(8,128)S(1)}, u32[]{:S(2)}) copy-start(f32[8,1440]{1,0:T(8,128)S(1)} %get-tuple-element.13) | copy-start | bytes 138244
  31.1 113.6 %copy-start.8 = (f32[8,1440]{1,0:T(8,128)}, f32[8,1440]{1,0:T(8,128)S(1)}, u32[]{:S(2)}) copy-start(f32[8,1440]{1,0:T(8,128)S(1)} %get-tuple-element.14) | copy-start | bytes 138244
  31.2 113.6 %copy-start.10 = (f32[8,1440]{1,0:T(8,128)}, f32[8,1440]{1,0:T(8,128)S(1)}, u32[]{:S(2)}) copy-start(f32[8,1440]{1,0:T(8,128)S(1)} %get-tuple-element.15) | copy-start | bytes 138244
  35.5 125.3 %all-to-all-start.2 = ((bf16[32,2,4480]{2,1,0:T(2,128)(2,1)}), bf16[32,2,4480]{2,1,0:T(2,128)(2,1)}, u32[]{:S(2)}, u32[]{:S(2)}) async-start(bf16[32,2,4480]{2,1,0:T(2,128)(2,1)} %reshape.358), calls=%async_computation.2 | async-start | bytes 1146880 | tf_op jit(solution)/shard_map/all_to_all | solution.py:104
  140.3 4.4 copy-start.1
  149.4 21.8 %copy-start.12 = (f32[640]{0:T(1024)S(1)}, f32[640]{0:T(1024)}, u32[]{:S(2)}) copy-start(f32[640]{0:T(1024)} %param.11) | copy-start | bytes 7684
  160.8 119.6 %all-to-all-start.1 = ((bf16[32,2,4480]{2,1,0:T(2,128)(2,1)}), bf16[32,2,4480]{2,1,0:T(2,128)(2,1)}, u32[]{:S(2)}, u32[]{:S(2)}) async-start(bf16[32,2,4480]{2,1,0:T(2,128)(2,1)} %reshape.360), calls=%async_computation.1 | async-start | bytes 1146880 | tf_op jit(solution)/shard_map/all_to_all | solution.py:103
  380.9 8.3 %copy-start.2 = (bf16[1,640,1440]{1,2,0:T(8,128)(2,1)S(1)}, bf16[1,640,1440]{1,2,0:T(8,128)(2,1)}, u32[]{:S(2)}) copy-start(bf16[1,640,1440]{1,2,0:T(8,128)(2,1)} %get-tuple-element.21) | copy-start | bytes 5529604
  380.9 8.3 %copy-start.7 = (f32[8,1440]{1,0:T(8,128)S(1)}, f32[8,1440]{1,0:T(8,128)}, u32[]{:S(2)}) copy-start(f32[8,1440]{1,0:T(8,128)} %copy-done.6) | copy-start | bytes 138244
  380.9 8.3 %copy-start.9 = (f32[8,1440]{1,0:T(8,128)S(1)}, f32[8,1440]{1,0:T(8,128)}, u32[]{:S(2)}) copy-start(f32[8,1440]{1,0:T(8,128)} %copy-done.8) | copy-start | bytes 138244
  380.9 8.3 %copy-start.11 = (f32[8,1440]{1,0:T(8,128)S(1)}, f32[8,1440]{1,0:T(8,128)}, u32[]{:S(2)}) copy-start(f32[8,1440]{1,0:T(8,128)} %copy-done.10) | copy-start | bytes 138244
  393.8 5.0 copy-start.3
  599.5 21.8 %all-to-all-start.4 = ((bf16[28,64,128]{2,0,1:T(8,128)(2,1)}), bf16[28,64,128]{2,0,1:T(8,128)(2,1)S(1)}, u32[]{:S(2)}, u32[]{:S(2)}) async-start(bf16[28,64,128]{2,0,1:T(8,128)(2,1)} %copy.129), calls=%async_computation.4 | async-start | bytes 1048576 | tf_op jit(solution)/shard_map/all_to_all | solution.py:122
where the time goes:
time: 629 us; the launch traced here: 623 us
  local copies, waits for them, and re-layouts  233 us (37%)
  other arithmetic  223 us (35%)
  blocking collectives  103 us (16%)
  starting transfers between devices  31.8 us (5%)
  waiting for transfers between devices  21.2 us (3%)
  matrix products  9.32 us (1%)
    scatter-add x3, other arithmetic, shards(): buffer_grad.at[:, cell_ref[member]]  189 us
    psum x1, blocking collectives, shards(): lax.psum(energy_part, ('band', 'chan')) / (C * K * lat_total) + epsilon  76.8 us
    gather x3, local copies, waits for them, and re-layouts, shards(): flattened[:, cell_ref[regrid_member]]  71.4 us
    unnamed x35, local copies, waits for them, and re-layouts  48.9 us
    all_to_all x1, blocking collectives, shards(): lax.all_to_all(moved_grad, 'band', split_axis=1, concat_axis=3, tiled=True)  26.4 us
    all_to_all x3, local copies, waits for them, and re-layouts, shards(): lax.all_to_all(moved_grad, 'band', split_axis=1, concat_axis=3, tiled=True)  20.2 us
    convert_element_type x2, local copies, waits for them, and re-layouts, amplitude_grad(): spectrum.astype(jnp.float32)  19 us
    convert_element_type x2, local copies, waits for them, and re-layouts, power_sums(): observed = target.astype(jnp.float32)  18.9 us
  transfers between devices with their start and end apart: 4, of which 2 were waited for; matrix products, arithmetic and copies ran while one was open for 26% of the time, Pallas kernels for 0%

commit v1 on v0

v1 whole, which is shorter than its diff:
```python
import functools
import math

import jax
import jax.numpy as jnp
import numpy as np
from jax import lax
from jax.experimental import pallas as pl
from jax.experimental.pallas import tpu as pltpu
from jax.sharding import PartitionSpec as P

C = 224
LON = 1440
K = 640
J = 3
NB = 128
LAT_DEV = 8
NBLK_DEV = 32
CAP = 2

LONP = 1536
TILE = 256
LO = CAP * NB
CP = 32
ROWS = LAT_DEV * CP

epsilon = 1e-06


def dft_table():
    wavenumber = np.arange(K, dtype=np.int64)[:, None]
    column = np.arange(LON, dtype=np.int64)[None, :]
    phase_count = wavenumber * column % LON
    phase_angle = np.float32(2.0 * math.pi / LON) * phase_count.astype(np.float32)
    norm_factor = np.float32(1.0 / math.sqrt(LON))
    table = np.stack([np.cos(phase_angle) * norm_factor, -np.sin(phase_angle) * norm_factor])
    table = table.astype(jnp.bfloat16).reshape(2 * K, LON)
    return np.pad(table, ((0, 0), (0, LONP - LON)))


def lat_weights(first_row, row_count, lat_total):
    row_index = first_row + jnp.arange(row_count, dtype=jnp.int32)
    latitude = (row_index.astype(jnp.float32) + 0.5) * (math.pi / lat_total) - 0.5 * math.pi
    return jnp.cos(latitude)


def pack_kernel(slot_ref, nodes_ref, out_ref):
    out_ref[...] = jnp.zeros_like(out_ref)
    for i in range(NBLK_DEV):
        slot = slot_ref[i]
        half = pl.ds(pl.multiple_of((slot & 1) * NB, NB), NB)
        out_ref[slot >> 1, :, half] = nodes_ref[:, i * NB : (i + 1) * NB]


def unpack_kernel(slot_ref, scale_ref, blocks_ref, out_ref):
    scale = scale_ref[0]
    for i in range(NBLK_DEV):
        slot = slot_ref[i]
        half = pl.ds(pl.multiple_of((slot & 1) * NB, NB), NB)
        block = blocks_ref[slot >> 1, :, half].astype(jnp.float32) * scale
        out_ref[:, i * NB : (i + 1) * NB] = block.astype(jnp.bfloat16)


def one_hot(ref_row):
    owner = ref_row >> 8
    place = ref_row & (LO - 1)
    rows = lax.broadcasted_iota(jnp.int32, (LO, ref_row.shape[1]), 0)
    return owner, (rows == place).astype(jnp.float32).astype(jnp.bfloat16)


def forward_kernel(owners, lat_ref, buf_ref, cell_ref, weight_ref, table_ref, target_ref,
                   spec_ref, sums_ref, nodes, grid):
    chans = buf_ref.shape[1]
    nodes[...] = jnp.zeros_like(nodes)
    for o in range(owners):
        nodes[o * CP : o * CP + chans, :] = buf_ref[o]

    def row(a, _):
        for t in range(LONP // TILE):
            cols = slice(t * TILE, (t + 1) * TILE)
            total = jnp.zeros((CP, TILE), jnp.float32)
            for m in range(J):
                refs = cell_ref[m, pl.ds(a, 1), cols]
                owner, hot = one_hot(refs)
                picked = jnp.dot(nodes[...], hot, preferred_element_type=jnp.float32)
                value = jnp.zeros((CP, TILE), jnp.float32)
                for o in range(owners):
                    value = jnp.where(owner == o, picked[o * CP : (o + 1) * CP], value)
                total = total + weight_ref[m, pl.ds(a, 1), cols] * value
            grid[pl.ds(pl.multiple_of(a * CP, CP), CP), cols] = total.astype(jnp.bfloat16)
        return 0

    lax.fori_loop(0, LAT_DEV, row, 0)
    spectrum = lax.dot_general(
        grid[...], table_ref[...], (((1,), (1,)), ((), ())), preferred_element_type=jnp.float32
    )
    spec_ref[...] = spectrum.astype(jnp.bfloat16)
    pred = jnp.zeros((CP, 2 * K), jnp.float32)
    true = jnp.zeros((CP, 2 * K), jnp.float32)
    cross = jnp.zeros((CP, 2 * K), jnp.float32)
    for a in range(LAT_DEV):
        s = spec_ref[a * CP : (a + 1) * CP, :].astype(jnp.float32)
        g = target_ref[a * CP : (a + 1) * CP, :].astype(jnp.float32)
        ws = lat_ref[a] * s
        pred = pred + ws * s
        cross = cross + ws * g
        true = true + lat_ref[a] * g * g
    sums_ref[0] = pred[:, :K] + pred[:, K:]
    sums_ref[1] = true[:, :K] + true[:, K:]
    sums_ref[2] = cross[:, :K] + cross[:, K:]


def backward_kernel(owners, lat_ref, cell_ref, weight_ref, table_ref, target_ref, spec_ref,
                    sums_ref, spec_weight_ref, out_ref, grads, total, gated):
    chans = out_ref.shape[1]
    pred_power, true_power, cross_sum = sums_ref[0], sums_ref[1], sums_ref[2]
    loss_scale = spec_weight_ref[...]
    amp_pred = jnp.sqrt(pred_power + epsilon)
    amp_true = jnp.sqrt(true_power + epsilon)
    d_pred = (
        loss_scale
        * (
            4.0 * amp_pred
            - 2.0 * amp_true
            - cross_sum * (1.0 / amp_true - amp_true / (amp_pred * amp_pred))
        )
        / (2.0 * amp_pred)
    )
    d_cross = -loss_scale * (amp_pred / amp_true + amp_true / amp_pred)
    for a in range(LAT_DEV):
        rows = slice(a * CP, (a + 1) * CP)
        for r in range(2):
            cols = slice(r * K, (r + 1) * K)
            s = spec_ref[rows, cols].astype(jnp.float32)
            g = target_ref[rows, cols].astype(jnp.float32)
            grads[rows, cols] = (lat_ref[a] * (2.0 * s * d_pred + g * d_cross)).astype(jnp.bfloat16)
    grid_grad = jnp.dot(grads[...], table_ref[...], preferred_element_type=jnp.float32)
    gated_grad = grid_grad
    total[...] = jnp.zeros_like(total)
    gated[...] = gated_grad

    def row(a, _):
        for t in range(LONP // TILE):
            cols = slice(t * TILE, (t + 1) * TILE)
            value = gated[pl.ds(pl.multiple_of(a * CP, CP), CP), cols]
            for m in range(J):
                refs = cell_ref[m, pl.ds(a, 1), cols]
                owner, hot = one_hot(refs)
                part = weight_ref[m, pl.ds(a, 1), cols] * value
                spread = jnp.concatenate(
                    [jnp.where(owner == o, part, 0.0).astype(jnp.bfloat16) for o in range(owners)],
                    axis=0,
                )
                total[...] += lax.dot_general(
                    spread, hot, (((1,), (1,)), ((), ())), preferred_element_type=jnp.float32
                )
        return 0

    lax.fori_loop(0, LAT_DEV, row, 0)
    for o in range(owners):
        out_ref[o] = total[o * CP : o * CP + chans, :].astype(jnp.bfloat16)


SMEM = pl.BlockSpec(memory_space=pltpu.SMEM)
VMEM = pl.BlockSpec(memory_space=pltpu.VMEM)
PARAMS = pltpu.CompilerParams(vmem_limit_bytes=40 * 1024 * 1024)


def shards(node_values, block_slot, cell_ref, cell_weight, target_spectrum, spec_weight):
    owners = lax.axis_size("band")
    band_index = lax.axis_index("band")
    samples, chans, nodes_local = node_values.shape
    lat_total = LAT_DEV * owners
    lat_weight = lat_weights(band_index * LAT_DEV, LAT_DEV, lat_total)
    table = jnp.asarray(dft_table())

    outgoing = pl.pallas_call(
        pack_kernel,
        out_shape=jax.ShapeDtypeStruct((owners, chans, LO), jnp.bfloat16),
        in_specs=[SMEM, VMEM],
        out_specs=VMEM,
        compiler_params=PARAMS,
        name="pack",
    )(block_slot, node_values[0])
    received = lax.all_to_all(outgoing, "band", split_axis=0, concat_axis=0, tiled=True)

    pad = ((0, 0), (0, 0), (0, LONP - LON))
    refs = jnp.pad(cell_ref, pad, constant_values=-1)
    weights = jnp.pad(cell_weight, pad)
    target = jnp.pad(
        jnp.transpose(target_spectrum[0].reshape(chans, LAT_DEV, 2 * K), (1, 0, 2)),
        ((0, 0), (0, CP - chans), (0, 0)),
    ).reshape(ROWS, 2 * K)

    spectrum, sums = pl.pallas_call(
        functools.partial(forward_kernel, owners),
        out_shape=(
            jax.ShapeDtypeStruct((ROWS, 2 * K), jnp.bfloat16),
            jax.ShapeDtypeStruct((3, CP, K), jnp.float32),
        ),
        in_specs=[SMEM] + [VMEM] * 5,
        out_specs=(VMEM, VMEM),
        scratch_shapes=[
            pltpu.VMEM((owners * CP, LO), jnp.bfloat16),
            pltpu.VMEM((ROWS, LONP), jnp.bfloat16),
        ],
        compiler_params=PARAMS,
        name="forward",
    )(lat_weight, received, refs, weights, table, target)

    sums = lax.psum(sums, "band")
    energy_part = jnp.sum(sums[1, :chans] * spec_weight[None, :])
    energy = lax.psum(energy_part, "chan") / (C * K * lat_total) + epsilon

    slot_grad = pl.pallas_call(
        functools.partial(backward_kernel, owners),
        out_shape=jax.ShapeDtypeStruct((owners, chans, LO), jnp.bfloat16),
        in_specs=[SMEM] + [VMEM] * 7,
        out_specs=VMEM,
        scratch_shapes=[
            pltpu.VMEM((ROWS, 2 * K), jnp.bfloat16),
            pltpu.VMEM((owners * CP, LO), jnp.float32),
            pltpu.VMEM((ROWS, LONP), jnp.float32),
        ],
        compiler_params=PARAMS,
        name="backward",
    )(lat_weight, refs, weights, table, target, spectrum, sums, spec_weight[None, :])

    returned = lax.all_to_all(slot_grad, "band", split_axis=0, concat_axis=0, tiled=True)
    node_grad = pl.pallas_call(
        unpack_kernel,
        out_shape=jax.ShapeDtypeStruct((chans, nodes_local), jnp.bfloat16),
        in_specs=[SMEM, SMEM, VMEM],
        out_specs=VMEM,
        compiler_params=PARAMS,
        name="unpack",
    )(block_slot, (1.0 / energy).reshape(1), returned)
    return node_grad[None]


def solution(mesh):
    in_specs = (
        P(None, "chan", "band"),
        P("band"),
        P(None, "band", None),
        P(None, "band", None),
        P(None, "chan", "band", None, None),
        P(),
    )
    out_specs = P(None, "chan", "band")
    return jax.shard_map(shards, mesh=mesh, in_specs=in_specs, out_specs=out_specs, check_vma=False)
```

time: 629 us -> 263 us (0.42)
  local copies, waits for them, and re-layouts: 233 us -> 9.05 us
  other arithmetic: 223 us -> 1.56 us
  waiting for transfers between devices: 21.2 us -> 154 us
  blocking collectives: 103 us -> 13.6 us
  Pallas kernels: 0 us -> 50.7 us
  starting transfers between devices: 31.8 us -> 18 us
  between operations: 1.35 us -> 14.2 us
  matrix products: 9.32 us -> 0 us
    scatter-add x3 -> x0, other arithmetic: 189 us -> none  [shards(): buffer_grad.at[:, cell_ref[member]]]
    psum x0 -> x1, waiting for transfers between devices: none -> 139 us  [shards(): sums = lax.psum(sums, 'band')]
    gather x5 -> x0, local copies, waits for them, and re-layouts: 72.1 us -> none  [the longest x3 71.4 us: shards(): flattened[:, cell_ref[regrid_member]]]
    psum x1, blocking collectives: 76.8 us -> 13.6 us  [shards(): energy = lax.psum(energy_part, 'chan') / (C * K * lat_total) + epsilon]
    convert_element_type x9 -> x0, local copies, waits for them, and re-layouts: 58.1 us -> none  [the longest x2 19 us: amplitude_grad(): spectrum.astype(jnp.float32)]
    pallas_call x0 -> x4, Pallas kernels: none -> 50.7 us  [the longest x1 24 us: shards(): pl.pallas_call(functools.partial(forward_kernel, owners), out_shape=(jax....]
    unnamed x35 -> x18, local copies, waits for them, and re-layouts: 48.9 us -> 6.79 us
    all_to_all x5 -> x0, local copies, waits for them, and re-layouts: 27.6 us -> none  [the longest x3 20.2 us: shards(): lax.all_to_all(moved_grad, 'band', split_axis=1, concat_axis=3, tiled=True)]
  transfers between devices with their start and end apart: 4 -> 3, of which waited for: 2 -> 2; matrix products, arithmetic and copies ran while one was open for 26% -> 1% of each run, Pallas kernels for 0% -> 0%
where the time goes in v1:
time: 263 us; the launch traced here: 262 us
  waiting for transfers between devices  154 us (59%)
  Pallas kernels  50.7 us (19%)
  starting transfers between devices  18 us (7%)
  between operations  14.2 us (5%)
  blocking collectives  13.6 us (5%)
  local copies, waits for them, and re-layouts  9.05 us (3%)
    psum x1, waiting for transfers between devices, shards(): sums = lax.psum(sums, 'band')  139 us
    pallas_call x1, Pallas kernels, shards(): pl.pallas_call(functools.partial(forward_kernel, owners), out_shape=(jax....  24 us
    pallas_call x1, Pallas kernels, shards(): pl.pallas_call(functools.partial(backward_kernel, owners), out_shape=jax....  23.9 us
    all_to_all x1, waiting for transfers between devices, shards(): lax.all_to_all(outgoing, 'band', split_axis=0, concat_axis=0, tiled=True)  15.2 us
    psum x1, blocking collectives, shards(): energy = lax.psum(energy_part, 'chan') / (C * K * lat_total) + epsilon  13.6 us
    all_to_all x1, starting transfers between devices, shards(): lax.all_to_all(outgoing, 'band', split_axis=0, concat_axis=0, tiled=True)  11.2 us
    unnamed x18, local copies, waits for them, and re-layouts  6.79 us
    all_to_all x1, starting transfers between devices, shards(): lax.all_to_all(slot_grad, 'band', split_axis=0, concat_axis=0, tiled=True)  6.76 us
  transfers between devices with their start and end apart: 3, of which 2 were waited for; matrix products, arithmetic and copies ran while one was open for 1% of the time, Pallas kernels for 0%

profile of v1, /device:TPU:32, one launch (start us, length us, event | category | flops | bytes accessed | tf_op | source)
XLA Modules:
  0.0 261.6 jit_solution(3016402480346567992)
XLA Ops:
  6.5 0.0 copy-start.3
  6.5 0.9 copy-done.3
  7.5 0.0 copy-start.4
  7.5 0.7 copy-done.4
  8.1 0.0 copy-start.6
  8.1 0.0 copy-start.7
  8.1 1.4 pack.1
  9.6 11.2 %all-to-all-start = ((bf16[32,28,256]{2,1,0:T(8,128)(2,1)}), bf16[32,28,256]{2,1,0:T(8,128)(2,1)S(1)}, u32[]{:S(2)}, u32[]{:S(2)}) async-start(bf16[32,28,256]{2,1,0:T(8,128)(2,1)} %pack.1), calls=%async_computation | async-start | bytes 1048576 | tf_op jit(solution)/shard_map/all_to_all | solution.py:185
  20.8 0.0 all-reduce.5.cloned.1.call-start
  20.8 2.1 reshape_squeeze.3
  22.9 0.1 copy.10
  23.0 0.0 copy-start.8
  23.1 0.0 copy-done.6
  23.1 0.0 copy-done.7
  23.2 15.2 %all-to-all-done.buf_ref = bf16[32,28,256]{2,1,0:T(8,128)(2,1)S(1)} async-done(((bf16[32,28,256]{2,1,0:T(8,128)(2,1)}), bf16[32,28,256]{2,1,0:T(8,128)(2,1)S(1)}, u32[]{:S(2)}, u32[]{:S(2)}) %all-to-all-start) | async-done | bytes 458784 | tf_op jit(solution)/shard_map/all_to_all | solution.py:185
  38.4 0.0 copy-start
  38.4 2.1 copy-done
  40.5 24.0 %forward.1 = (bf16[256,1280]{1,0:T(8,128)(2,1)S(1)}, f32[3,32,640]{2,1,0:T(8,128)}) custom-call(f32[8]{0:T(128)S(1)} %add_cosine_fusion.lat_ref, bf16[32,28,256]{2,1,0:T(8,128)(2,1)S(1)} %all-to-all-done.buf_ref, s32[3,8,1536]{2,1,0:T(8,128)S(1)} %pad.12.cell_ref, f32[3,8,1536]{2,1,0:T(8,128)S(1)} %pad.13.weight_ref, bf16[1280,1536]{1,0:T(8,128)(2,1)S(1)} %copy-done, ...), custom_call_target="tpu_custom_call" | custom-call | tf_op jit(solution)/shard_map/forward/pallas_call | solution.py:195
  64.6 0.0 copy-start.5
  64.6 0.0 all-reduce.5.cloned.1.call-update
  64.6 0.0 copy-done.8
  64.6 139.2 %all-reduce.5.cloned.1.call-done.sums_ref = f32[3,32,640]{2,1,0:T(8,128)} async-done(((f32[3,32,640]{2,1,0:T(8,128)}), f32[3,32,640]{2,1,0:T(8,128)}) %all-reduce.5.cloned.1.call-update) | async-done | bytes 245776 | tf_op jit(solution)/shard_map/psum | solution.py:211
  203.8 0.0 copy-start.1
  203.8 2.1 copy-done.1
  205.9 0.0 copy-start.2
  205.9 0.9 copy-done.2
  206.9 23.9 %backward.1 = bf16[32,28,256]{2,1,0:T(8,128)(2,1)} custom-call(f32[8]{0:T(128)S(1)} %add_cosine_fusion.lat_ref, s32[3,8,1536]{2,1,0:T(8,128)S(1)} %pad.12.cell_ref, f32[3,8,1536]{2,1,0:T(8,128)S(1)} %pad.13.weight_ref, bf16[1280,1536]{1,0:T(8,128)(2,1)S(1)} %copy-done.1, bf16[256,1280]{1,0:T(8,128)(2,1)S(1)} %bitcast.14, ...), custom_call_target="tpu_custom_call" | custom-call | tf_op jit(solution)/shard_map/backward/pallas_call | solution.py:215
  230.8 6.8 %all-to-all-start.1 = ((bf16[32,28,256]{2,1,0:T(8,128)(2,1)}), bf16[32,28,256]{2,1,0:T(8,128)(2,1)S(1)}, u32[]{:S(2)}, u32[]{:S(2)}) async-start(bf16[32,28,256]{2,1,0:T(8,128)(2,1)} %backward.1), calls=%async_computation.1 | async-start | bytes 1048576 | tf_op jit(solution)/shard_map/all_to_all | solution.py:229
  237.6 1.5 fusion.1
  239.1 13.6 %psum.15 = f32[]{:T(128)} all-reduce(f32[]{:T(128)} %fusion.1), channel_id=1, replica_groups=mesh['band'=32,'chan'=8] {'chan'}, use_global_device_ids=true, to_apply=%region_2.3 | all-reduce | flops 1 | bytes 8 | tf_op jit(solution)/shard_map/psum | solution.py:213
  253.4 0.0 all-to-all-done.1.blocks_ref
  253.4 0.0 copy-done.5
  253.4 1.3 unpack.1
  (5 shorter events, 0.1 us)
Async XLA Ops:
  6.5 0.9 copy-start.3
  7.5 0.7 copy-start.4
  8.1 15.0 %copy-start.6 = (s32[3,8,1440]{2,1,0:T(8,128)S(1)}, s32[3,8,1440]{2,1,0:T(8,128)}, u32[]{:S(2)}) copy-start(s32[3,8,1440]{2,1,0:T(8,128)} %param.9) | copy-start | bytes 414724
  8.1 15.0 %copy-start.7 = (f32[3,8,1440]{2,1,0:T(8,128)S(1)}, f32[3,8,1440]{2,1,0:T(8,128)}, u32[]{:S(2)}) copy-start(f32[3,8,1440]{2,1,0:T(8,128)} %param.10) | copy-start | bytes 414724
  9.6 28.8 %all-to-all-start = ((bf16[32,28,256]{2,1,0:T(8,128)(2,1)}), bf16[32,28,256]{2,1,0:T(8,128)(2,1)S(1)}, u32[]{:S(2)}, u32[]{:S(2)}) async-start(bf16[32,28,256]{2,1,0:T(8,128)(2,1)} %pack.1), calls=%async_computation | async-start | bytes 1048576 | tf_op jit(solution)/shard_map/all_to_all | solution.py:185
  20.8 183.0 %all-reduce.5.cloned.1.call-start = ((), (), s32[]{:S(2)}) async-start(), calls=%async_computation.2 | async-start | bytes 491520 | tf_op jit(solution)/shard_map/psum | solution.py:211
  23.0 41.5 %copy-start.8 = (f32[640]{0:T(1024)S(1)}, f32[640]{0:T(1024)}, u32[]{:S(2)}) copy-start(f32[640]{0:T(1024)} %param.12) | copy-start | bytes 7684
  38.4 2.1 copy-start
  64.6 188.8 %copy-start.5 = (s32[32]{0:T(128)S(1)}, s32[32]{0:T(128)}, u32[]{:S(2)}) copy-start(s32[32]{0:T(128)} %slot_ref.3) | copy-start | bytes 388
  203.8 2.1 copy-start.1
  205.9 0.9 copy-start.2
  230.8 22.6 %all-to-all-start.1 = ((bf16[32,28,256]{2,1,0:T(8,128)(2,1)}), bf16[32,28,256]{2,1,0:T(8,128)(2,1)S(1)}, u32[]{:S(2)}, u32[]{:S(2)}) async-start(bf16[32,28,256]{2,1,0:T(8,128)(2,1)} %backward.1), calls=%async_computation.1 | async-start | bytes 1048576 | tf_op jit(solution)/shard_map/all_to_all | solution.py:229
Sparse Core Ops, SparseCore 0:
  64.7 139.0 all-reduce.4

commit v2 on v1

--- a/solution.py
+++ b/solution.py
@@ -52,13 +52,43 @@
         out_ref[slot >> 1, :, half] = nodes_ref[:, i * NB : (i + 1) * NB]
 
 
-def unpack_kernel(slot_ref, scale_ref, blocks_ref, out_ref):
-    scale = scale_ref[0]
+def unpack_kernel(slot_ref, blocks_ref, out_ref):
     for i in range(NBLK_DEV):
         slot = slot_ref[i]
         half = pl.ds(pl.multiple_of((slot & 1) * NB, NB), NB)
-        block = blocks_ref[slot >> 1, :, half].astype(jnp.float32) * scale
-        out_ref[:, i * NB : (i + 1) * NB] = block.astype(jnp.bfloat16)
+        out_ref[:, i * NB : (i + 1) * NB] = blocks_ref[slot >> 1, :, half]
+
+
+def true_kernel(lat_ref, spec_weight_ref, target_ref, true_ref, energy_ref):
+    true = jnp.zeros((CP, 2 * K), jnp.float32)
+    for a in range(LAT_DEV):
+        g = target_ref[a * CP : (a + 1) * CP, :].astype(jnp.float32)
+        true = true + lat_ref[a] * g * g
+    true = true[:, :K] + true[:, K:]
+    true_ref[...] = true
+    energy = jnp.sum(true * spec_weight_ref[...], axis=(0, 1), keepdims=True)
+    energy_ref[...] = jnp.broadcast_to(energy, energy_ref.shape)
+
+
+def middle_kernel(scale, parts_ref, spec_weight_ref, out_ref):
+    sums = jnp.sum(parts_ref[...], axis=0)
+    pred_power, true_power, cross_sum = sums[0:1], sums[1:2], sums[2:3]
+    energy = sums[3:4] * scale + epsilon
+    loss_scale = spec_weight_ref[...] / energy
+    amp_pred = jnp.sqrt(pred_power + epsilon)
+    amp_true = jnp.sqrt(true_power + epsilon)
+    d_pred = (
+        loss_scale
+        * (
+            4.0 * amp_pred
+            - 2.0 * amp_true
+            - cross_sum * (1.0 / amp_true - amp_true / (amp_pred * amp_pred))
+        )
+        / (2.0 * amp_pred)
+    )
+    d_cross = -loss_scale * (amp_pred / amp_true + amp_true / amp_pred)
+    both = jnp.concatenate([d_pred, d_cross], axis=0)
+    out_ref[...] = jnp.broadcast_to(both[None], out_ref.shape)
 
 
 def one_hot(ref_row):
@@ -69,7 +99,7 @@
 
 
 def forward_kernel(owners, lat_ref, buf_ref, cell_ref, weight_ref, table_ref, target_ref,
-                   spec_ref, sums_ref, nodes, grid):
+                   true_ref, energy_ref, spec_ref, sums_ref, nodes, grid):
     chans = buf_ref.shape[1]
     nodes[...] = jnp.zeros_like(nodes)
     for o in range(owners):
@@ -96,7 +126,6 @@
     )
     spec_ref[...] = spectrum.astype(jnp.bfloat16)
     pred = jnp.zeros((CP, 2 * K), jnp.float32)
-    true = jnp.zeros((CP, 2 * K), jnp.float32)
     cross = jnp.zeros((CP, 2 * K), jnp.float32)
     for a in range(LAT_DEV):
         s = spec_ref[a * CP : (a + 1) * CP, :].astype(jnp.float32)
@@ -104,29 +133,17 @@
         ws = lat_ref[a] * s
         pred = pred + ws * s
         cross = cross + ws * g
-        true = true + lat_ref[a] * g * g
-    sums_ref[0] = pred[:, :K] + pred[:, K:]
-    sums_ref[1] = true[:, :K] + true[:, K:]
-    sums_ref[2] = cross[:, :K] + cross[:, K:]
+    energy = jnp.sum(energy_ref[...], axis=0)[0:1, 0:1]
+    sums_ref[:, 0, :] = pred[:, :K] + pred[:, K:]
+    sums_ref[:, 1, :] = true_ref[...]
+    sums_ref[:, 2, :] = cross[:, :K] + cross[:, K:]
+    sums_ref[:, 3, :] = jnp.broadcast_to(energy, (CP, K))
 
 
 def backward_kernel(owners, lat_ref, cell_ref, weight_ref, table_ref, target_ref, spec_ref,
-                    sums_ref, spec_weight_ref, out_ref, grads, total, gated):
+                    factor_ref, out_ref, grads, total, gated):
     chans = out_ref.shape[1]
-    pred_power, true_power, cross_sum = sums_ref[0], sums_ref[1], sums_ref[2]
-    loss_scale = spec_weight_ref[...]
-    amp_pred = jnp.sqrt(pred_power + epsilon)
-    amp_true = jnp.sqrt(true_power + epsilon)
-    d_pred = (
-        loss_scale
-        * (
-            4.0 * amp_pred
-            - 2.0 * amp_true
-            - cross_sum * (1.0 / amp_true - amp_true / (amp_pred * amp_pred))
-        )
-        / (2.0 * amp_pred)
-    )
-    d_cross = -loss_scale * (amp_pred / amp_true + amp_true / amp_pred)
+    d_pred, d_cross = factor_ref[:, 0, :], factor_ref[:, 1, :]
     for a in range(LAT_DEV):
         rows = slice(a * CP, (a + 1) * CP)
         for r in range(2):
@@ -135,9 +152,8 @@
             g = target_ref[rows, cols].astype(jnp.float32)
             grads[rows, cols] = (lat_ref[a] * (2.0 * s * d_pred + g * d_cross)).astype(jnp.bfloat16)
     grid_grad = jnp.dot(grads[...], table_ref[...], preferred_element_type=jnp.float32)
-    gated_grad = grid_grad
     total[...] = jnp.zeros_like(total)
-    gated[...] = gated_grad
+    gated[...] = grid_grad
 
     def row(a, _):
         for t in range(LONP // TILE):
@@ -166,6 +182,15 @@
 PARAMS = pltpu.CompilerParams(vmem_limit_bytes=40 * 1024 * 1024)
 
 
+def exchange(blocks, axis):
+    return lax.all_to_all(blocks, axis, split_axis=0, concat_axis=0, tiled=True)
+
+
+def everyone(block, axis):
+    count = lax.axis_size(axis)
+    return exchange(jnp.broadcast_to(block[None], (count,) + block.shape), axis)
+
+
 def shards(node_values, block_slot, cell_ref, cell_weight, target_spectrum, spec_weight):
     owners = lax.axis_size("band")
     band_index = lax.axis_index("band")
@@ -182,7 +207,7 @@
         compiler_params=PARAMS,
         name="pack",
     )(block_slot, node_values[0])
-    received = lax.all_to_all(outgoing, "band", split_axis=0, concat_axis=0, tiled=True)
+    received = exchange(outgoing, "band")
 
     pad = ((0, 0), (0, 0), (0, LONP - LON))
     refs = jnp.pad(cell_ref, pad, constant_values=-1)
@@ -192,13 +217,26 @@
         ((0, 0), (0, CP - chans), (0, 0)),
     ).reshape(ROWS, 2 * K)
 
+    true_part, energy_part = pl.pallas_call(
+        true_kernel,
+        out_shape=(
+            jax.ShapeDtypeStruct((CP, K), jnp.float32),
+            jax.ShapeDtypeStruct((8, 128), jnp.float32),
+        ),
+        in_specs=[SMEM, VMEM, VMEM],
+        out_specs=(VMEM, VMEM),
+        compiler_params=PARAMS,
+        name="true_power",
+    )(lat_weight, spec_weight[None, :], target)
+    energies = everyone(energy_part, "chan")
+
     spectrum, sums = pl.pallas_call(
         functools.partial(forward_kernel, owners),
         out_shape=(
             jax.ShapeDtypeStruct((ROWS, 2 * K), jnp.bfloat16),
-            jax.ShapeDtypeStruct((3, CP, K), jnp.float32),
+            jax.ShapeDtypeStruct((CP, 4, K), jnp.float32),
         ),
-        in_specs=[SMEM] + [VMEM] * 5,
+        in_specs=[SMEM] + [VMEM] * 7,
         out_specs=(VMEM, VMEM),
         scratch_shapes=[
             pltpu.VMEM((owners * CP, LO), jnp.bfloat16),
@@ -206,16 +244,23 @@
         ],
         compiler_params=PARAMS,
         name="forward",
-    )(lat_weight, received, refs, weights, table, target)
-
-    sums = lax.psum(sums, "band")
-    energy_part = jnp.sum(sums[1, :chans] * spec_weight[None, :])
-    energy = lax.psum(energy_part, "chan") / (C * K * lat_total) + epsilon
+    )(lat_weight, received, refs, weights, table, target, true_part, energies)
+
+    parts = exchange(sums, "band")
+    factors = pl.pallas_call(
+        functools.partial(middle_kernel, 1.0 / (C * K * lat_total)),
+        out_shape=jax.ShapeDtypeStruct((owners, 2, K), jnp.float32),
+        in_specs=[VMEM, VMEM],
+        out_specs=VMEM,
+        compiler_params=PARAMS,
+        name="middle",
+    )(parts, spec_weight[None, :])
+    factors = exchange(factors, "band")
 
     slot_grad = pl.pallas_call(
         functools.partial(backward_kernel, owners),
         out_shape=jax.ShapeDtypeStruct((owners, chans, LO), jnp.bfloat16),
-        in_specs=[SMEM] + [VMEM] * 7,
+        in_specs=[SMEM] + [VMEM] * 6,
         out_specs=VMEM,
         scratch_shapes=[
             pltpu.VMEM((ROWS, 2 * K), jnp.bfloat16),
@@ -224,17 +269,17 @@
         ],
         compiler_params=PARAMS,
         name="backward",
-    )(lat_weight, refs, weights, table, target, spectrum, sums, spec_weight[None, :])
-
-    returned = lax.all_to_all(slot_grad, "band", split_axis=0, concat_axis=0, tiled=True)
+    )(lat_weight, refs, weights, table, target, spectrum, factors)
+
+    returned = exchange(slot_grad, "band")
     node_grad = pl.pallas_call(
         unpack_kernel,
         out_shape=jax.ShapeDtypeStruct((chans, nodes_local), jnp.bfloat16),
-        in_specs=[SMEM, SMEM, VMEM],
+        in_specs=[SMEM, VMEM],
         out_specs=VMEM,
         compiler_params=PARAMS,
         name="unpack",
-    )(block_slot, (1.0 / energy).reshape(1), returned)
+    )(block_slot, returned)
     return node_grad[None]
 
 

time: 263 us -> 145 us (0.55)
  waiting for transfers between devices: 154 us -> 21.5 us
  blocking collectives: 13.6 us -> 51.1 us
  between operations: 14.2 us -> 0.13 us
  local copies, waits for them, and re-layouts: 9.05 us -> 5.76 us
    psum x1 -> x0, waiting for transfers between devices: 139 us -> none  [shards(): sums = lax.psum(sums, 'band')]
    all_to_all x0 -> x3, blocking collectives: none -> 51.1 us  [exchange(): return lax.all_to_all(blocks, axis, split_axis=0, concat_axis=0, tiled=True)]
    psum x1 -> x0, blocking collectives: 13.6 us -> none  [shards(): energy = lax.psum(energy_part, 'chan') / (C * K * lat_total) + epsilon]
    all_to_all x2, waiting for transfers between devices: 15.2 us -> 21.5 us  [exchange(): return lax.all_to_all(blocks, axis, split_axis=0, concat_axis=0, tiled=True)]
    unnamed x18 -> x12, local copies, waits for them, and re-layouts: 6.79 us -> 2.13 us
  transfers between devices with their start and end apart: 3 -> 2, of which waited for: 2 -> 2; matrix products, arithmetic and copies ran while one was open for 1% -> 0% of each run, Pallas kernels for 0% -> 1%
where the time goes in v2:
time: 145 us; the launch traced here: 144 us
  blocking collectives  51.1 us (35%)
  Pallas kernels  50.2 us (35%)
  waiting for transfers between devices  21.5 us (15%)
  starting transfers between devices  15.7 us (11%)
  local copies, waits for them, and re-layouts  5.76 us (4%)
    all_to_all x3, blocking collectives, exchange(): return lax.all_to_all(blocks, axis, split_axis=0, concat_axis=0, tiled=True)  51.1 us
    pallas_call x1, Pallas kernels, shards(): pl.pallas_call(functools.partial(forward_kernel, owners), out_shape=(jax....  23.4 us
    pallas_call x1, Pallas kernels, shards(): pl.pallas_call(functools.partial(backward_kernel, owners), out_shape=jax....  23 us
    all_to_all x2, waiting for transfers between devices, exchange(): return lax.all_to_all(blocks, axis, split_axis=0, concat_axis=0, tiled=True)  21.5 us
    all_to_all x2, starting transfers between devices, exchange(): return lax.all_to_all(blocks, axis, split_axis=0, concat_axis=0, tiled=True)  15.7 us
  transfers between devices with their start and end apart: 2, of which 2 were waited for; matrix products, arithmetic and copies ran while one was open for 0% of the time, Pallas kernels for 1%

profile of v2, /device:TPU:32, one launch (start us, length us, event | category | flops | bytes accessed | tf_op | source)
XLA Modules:
  0.0 144.5 jit_solution(16121205350282747752)
XLA Ops:
  0.0 0.0 copy-start.3
  0.0 0.0 copy-start.2
  0.0 0.0 copy-start.4
  0.0 0.0 copy-start.5
  0.1 0.8 broadcast_in_dim.6.spec_weight_ref
  0.8 2.1 %reshape_squeeze.3 = bf16[28,8,1280]{2,1,0:T(8,128)(2,1)S(1)} reshape(bf16[1,28,8,2,640]{4,3,2,1,0:T(2,128)(2,1)} %param.11) | data formatting | bytes 1146880 | tf_op jit(solution)/shard_map/reshape;squeeze | solution.py:216
  2.9 0.1 copy.10
  3.1 0.9 true_power.1
  4.0 0.6 broadcast_in_dim.14
  4.6 4.5 %all-to-all-start.1 = ((f32[8,8,128]{2,1,0:T(8,128)}), f32[8,8,128]{2,1,0:T(8,128)S(1)}, u32[]{:S(2)}, u32[]{:S(2)}) async-start(f32[8,8,128]{2,1,0:T(8,128)} %broadcast_in_dim.14), calls=%async_computation.1 | async-start | bytes 65536 | tf_op jit(solution)/shard_map/all_to_all | solution.py:186
  9.1 0.0 copy-done.3
  9.1 0.0 copy-done.2
  9.1 1.4 pack.1
  10.5 4.0 %all-to-all-done.1.energy_ref = f32[8,8,128]{2,1,0:T(8,128)S(1)} async-done(((f32[8,8,128]{2,1,0:T(8,128)}), f32[8,8,128]{2,1,0:T(8,128)S(1)}, u32[]{:S(2)}, u32[]{:S(2)}) %all-to-all-start.1) | async-done | bytes 32800 | tf_op jit(solution)/shard_map/all_to_all | solution.py:186
  14.5 11.2 %all-to-all-start = ((bf16[32,28,256]{2,1,0:T(8,128)(2,1)}), bf16[32,28,256]{2,1,0:T(8,128)(2,1)S(1)}, u32[]{:S(2)}, u32[]{:S(2)}) async-start(bf16[32,28,256]{2,1,0:T(8,128)(2,1)} %pack.1), calls=%async_computation | async-start | bytes 1048576 | tf_op jit(solution)/shard_map/all_to_all | solution.py:186
  25.7 0.0 copy-done.4
  25.8 0.0 copy-done.5
  25.8 17.5 %all-to-all-done.buf_ref = bf16[32,28,256]{2,1,0:T(8,128)(2,1)S(1)} async-done(((bf16[32,28,256]{2,1,0:T(8,128)(2,1)}), bf16[32,28,256]{2,1,0:T(8,128)(2,1)S(1)}, u32[]{:S(2)}, u32[]{:S(2)}) %all-to-all-start) | async-done | bytes 458784 | tf_op jit(solution)/shard_map/all_to_all | solution.py:186
  43.3 0.0 copy-start
  43.3 2.1 %copy-done = bf16[1280,1536]{1,0:T(8,128)(2,1)S(1)} copy-done((bf16[1280,1536]{1,0:T(8,128)(2,1)S(1)}, bf16[1280,1536]{1,0:T(8,128)(2,1)}, u32[]{:S(2)}) %copy-start) | copy-done | bytes 3932184
  45.4 0.0 copy-start.1
  45.4 23.4 %forward.1 = (bf16[256,1280]{1,0:T(8,128)(2,1)S(1)}, f32[32,4,640]{2,1,0:T(4,128)S(1)}) custom-call(f32[8]{0:T(128)S(1)} %add_cosine_fusion.lat_ref, bf16[32,28,256]{2,1,0:T(8,128)(2,1)S(1)} %all-to-all-done.buf_ref, s32[3,8,1536]{2,1,0:T(8,128)S(1)} %pad.12.cell_ref, f32[3,8,1536]{2,1,0:T(8,128)S(1)} %pad.13.weight_ref, bf16[1280,1536]{1,0:T(8,128)(2,1)S(1)} %copy-done, ...), custom_call_target="tpu_custom_call" | custom-call | tf_op jit(solution)/shard_map/forward/pallas_call | solution.py:233
  68.8 17.5 %all_to_all.25.parts_ref = f32[32,4,640]{2,1,0:T(4,128)S(1)} all-to-all(f32[32,4,640]{2,1,0:T(4,128)S(1)} %get-tuple-element.12), channel_id=1, replica_groups=mesh['band'=32,'chan'=8] {'band'}, dimensions={0} | all-to-all | bytes 655360 | tf_op jit(solution)/shard_map/all_to_all | solution.py:186
  86.3 0.1 middle.1
  86.4 14.5 %all_to_all.26.factor_ref = f32[32,2,640]{2,1,0:T(2,128)S(1)} all-to-all(f32[32,2,640]{2,1,0:T(2,128)S(1)} %middle.1), channel_id=1, replica_groups=mesh['band'=32,'chan'=8] {'band'}, dimensions={0} | all-to-all | bytes 327680 | tf_op jit(solution)/shard_map/all_to_all | solution.py:186
  101.0 0.0 copy-done.1
  101.0 23.0 %backward.1 = bf16[32,28,256]{2,1,0:T(8,128)(2,1)S(1)} custom-call(f32[8]{0:T(128)S(1)} %add_cosine_fusion.lat_ref, s32[3,8,1536]{2,1,0:T(8,128)S(1)} %pad.12.cell_ref, f32[3,8,1536]{2,1,0:T(8,128)S(1)} %pad.13.weight_ref, bf16[1280,1536]{1,0:T(8,128)(2,1)S(1)} %copy-done.1, bf16[256,1280]{1,0:T(8,128)(2,1)S(1)} %bitcast.8, ...), custom_call_target="tpu_custom_call" | custom-call | tf_op jit(solution)/shard_map/backward/pallas_call | solution.py:260
  124.0 19.1 %all_to_all.27.blocks_ref = bf16[32,28,256]{2,1,0:T(8,128)(2,1)S(1)} all-to-all(bf16[32,28,256]{2,1,0:T(8,128)(2,1)S(1)} %backward.1), channel_id=1, replica_groups=mesh['band'=32,'chan'=8] {'band'}, dimensions={0} | all-to-all | bytes 917504 | tf_op jit(solution)/shard_map/all_to_all | solution.py:186
  143.1 1.4 unpack.1
  (4 shorter events, 0.1 us)
Async XLA Ops:
  0.0 9.1 %copy-start.3 = (s32[32]{0:T(128)S(1)}, s32[32]{0:T(128)}, u32[]{:S(2)}) copy-start(s32[32]{0:T(128)} %slot_ref.3) | copy-start | bytes 388
  0.0 9.1 %copy-start.2 = (bf16[1,28,4096]{2,1,0:T(8,128)(2,1)S(1)}, bf16[1,28,4096]{2,1,0:T(8,128)(2,1)}, u32[]{:S(2)}) copy-start(bf16[1,28,4096]{2,1,0:T(8,128)(2,1)} %param.7) | copy-start | bytes 688132
  0.0 25.7 %copy-start.4 = (s32[3,8,1440]{2,1,0:T(8,128)S(1)}, s32[3,8,1440]{2,1,0:T(8,128)}, u32[]{:S(2)}) copy-start(s32[3,8,1440]{2,1,0:T(8,128)} %param.9) | copy-start | bytes 414724
  0.0 25.8 %copy-start.5 = (f32[3,8,1440]{2,1,0:T(8,128)S(1)}, f32[3,8,1440]{2,1,0:T(8,128)}, u32[]{:S(2)}) copy-start(f32[3,8,1440]{2,1,0:T(8,128)} %param.10) | copy-start | bytes 414724
  4.6 9.9 %all-to-all-start.1 = ((f32[8,8,128]{2,1,0:T(8,128)}), f32[8,8,128]{2,1,0:T(8,128)S(1)}, u32[]{:S(2)}, u32[]{:S(2)}) async-start(f32[8,8,128]{2,1,0:T(8,128)} %broadcast_in_dim.14), calls=%async_computation.1 | async-start | bytes 65536 | tf_op jit(solution)/shard_map/all_to_all | solution.py:186
  14.5 28.8 %all-to-all-start = ((bf16[32,28,256]{2,1,0:T(8,128)(2,1)}), bf16[32,28,256]{2,1,0:T(8,128)(2,1)S(1)}, u32[]{:S(2)}, u32[]{:S(2)}) async-start(bf16[32,28,256]{2,1,0:T(8,128)(2,1)} %pack.1), calls=%async_computation | async-start | bytes 1048576 | tf_op jit(solution)/shard_map/all_to_all | solution.py:186
  43.3 2.1 %copy-start = (bf16[1280,1536]{1,0:T(8,128)(2,1)S(1)}, bf16[1280,1536]{1,0:T(8,128)(2,1)}, u32[]{:S(2)}) copy-start(bf16[1280,1536]{1,0:T(8,128)(2,1)} %constant.24.clone.table_ref) | copy-start | bytes 11796484
  45.4 55.5 %copy-start.1 = (bf16[1280,1536]{1,0:T(8,128)(2,1)S(1)}, bf16[1280,1536]{1,0:T(8,128)(2,1)}, u32[]{:S(2)}) copy-start(bf16[1280,1536]{1,0:T(8,128)(2,1)} %constant.24.clone.table_ref) | copy-start | bytes 11796484

commit v3 on v2

--- a/solution.py
+++ b/solution.py
@@ -22,6 +22,13 @@
 TILE = 256
 LO = CAP * NB
 CP = 32
+MAIN = LON - LON % TILE
+REST = LON - MAIN
+CELL_ROWS = LAT_DEV + 1
+CHANS = 28
+HALF = 4
+BODY = CHANS - HALF
+PAIR = 2 * CHANS
 ROWS = LAT_DEV * CP
 
 epsilon = 1e-06
@@ -98,31 +105,59 @@
     return owner, (rows == place).astype(jnp.float32).astype(jnp.bfloat16)
 
 
-def forward_kernel(owners, lat_ref, buf_ref, cell_ref, weight_ref, table_ref, target_ref,
-                   true_ref, energy_ref, spec_ref, sums_ref, nodes, grid):
-    chans = buf_ref.shape[1]
-    nodes[...] = jnp.zeros_like(nodes)
-    for o in range(owners):
-        nodes[o * CP : o * CP + chans, :] = buf_ref[o]
+def shared_owner(owner):
+    first = lax.broadcasted_iota(jnp.int32, (2 * HALF, owner.shape[1]), 0) < HALF
+    wanted = jnp.where(first, 0, 1)
+    return jnp.where((owner & 1) == wanted, owner >> 1, -1)
+
+
+def forward_kernel(owners, lat_ref, buf_ref, cell_ref, weight_ref, table_hbm, target_ref,
+                   true_ref, *refs):
+    energy_refs = refs[:-8]
+    spec_ref, sums_ref, staged, nodes, grid, tail, table_ref, table_sem = refs[-8:]
+    table_copy = pltpu.make_async_copy(table_hbm, table_ref, table_sem)
+    table_copy.start()
+    for p in range(owners // 2):
+        even = buf_ref[2 * p].astype(jnp.float32)
+        odd = buf_ref[2 * p + 1].astype(jnp.float32)
+        staged[p * PAIR : p * PAIR + BODY, :] = even[:BODY]
+        shared = jnp.concatenate([even[BODY:], odd[BODY:]], axis=0)
+        staged[p * PAIR + BODY : p * PAIR + BODY + 2 * HALF, :] = shared
+        staged[p * PAIR + BODY + 2 * HALF : (p + 1) * PAIR, :] = odd[:BODY]
+    nodes[...] = staged[...].astype(jnp.bfloat16)
 
     def row(a, _):
-        for t in range(LONP // TILE):
+        for t in range(MAIN // TILE):
             cols = slice(t * TILE, (t + 1) * TILE)
             total = jnp.zeros((CP, TILE), jnp.float32)
             for m in range(J):
-                refs = cell_ref[m, pl.ds(a, 1), cols]
-                owner, hot = one_hot(refs)
+                owner, hot = one_hot(cell_ref[m, pl.ds(a, 1), cols])
+                shared = shared_owner(owner)
                 picked = jnp.dot(nodes[...], hot, preferred_element_type=jnp.float32)
-                value = jnp.zeros((CP, TILE), jnp.float32)
-                for o in range(owners):
-                    value = jnp.where(owner == o, picked[o * CP : (o + 1) * CP], value)
+                body = jnp.zeros((BODY, TILE), jnp.float32)
+                half = jnp.zeros((2 * HALF, TILE), jnp.float32)
+                for p in range(owners // 2):
+                    block = picked[p * PAIR : (p + 1) * PAIR]
+                    body = jnp.where(owner == 2 * p, block[:BODY], body)
+                    half = jnp.where(shared == p, block[BODY : BODY + 2 * HALF], half)
+                    body = jnp.where(owner == 2 * p + 1, block[BODY + 2 * HALF :], body)
+                value = jnp.concatenate([body, half + pltpu.roll(half, HALF, 0)], axis=0)
                 total = total + weight_ref[m, pl.ds(a, 1), cols] * value
             grid[pl.ds(pl.multiple_of(a * CP, CP), CP), cols] = total.astype(jnp.bfloat16)
         return 0
 
-    lax.fori_loop(0, LAT_DEV, row, 0)
+    lax.fori_loop(0, CELL_ROWS, row, 0)
+    rest = grid[ROWS : ROWS + CP, :].astype(jnp.float32)
+    for a in range(LAT_DEV):
+        piece = rest[:, a * REST : (a + 1) * REST]
+        piece = jnp.concatenate([piece, jnp.zeros((CP, TILE - REST), jnp.float32)], axis=1)
+        tail[a * CP : (a + 1) * CP, :] = piece.astype(jnp.bfloat16)
+    table_copy.wait()
+    contract = (((1,), (1,)), ((), ()))
     spectrum = lax.dot_general(
-        grid[...], table_ref[...], (((1,), (1,)), ((), ())), preferred_element_type=jnp.float32
+        grid[:ROWS, :], table_ref[:, :MAIN], contract, preferred_element_type=jnp.float32
+    ) + lax.dot_general(
+        tail[...], table_ref[:, MAIN:], contract, preferred_element_type=jnp.float32
     )
     spec_ref[...] = spectrum.astype(jnp.bfloat16)
     pred = jnp.zeros((CP, 2 * K), jnp.float32)
@@ -133,7 +168,9 @@
         ws = lat_ref[a] * s
         pred = pred + ws * s
         cross = cross + ws * g
-    energy = jnp.sum(energy_ref[...], axis=0)[0:1, 0:1]
+    energy = energy_refs[0][0:1, 0:1]
+    for energy_ref in energy_refs[1:]:
+        energy = energy + energy_ref[0:1, 0:1]
     sums_ref[:, 0, :] = pred[:, :K] + pred[:, K:]
     sums_ref[:, 1, :] = true_ref[...]
     sums_ref[:, 2, :] = cross[:, :K] + cross[:, K:]
@@ -142,7 +179,6 @@
 
 def backward_kernel(owners, lat_ref, cell_ref, weight_ref, table_ref, target_ref, spec_ref,
                     factor_ref, out_ref, grads, total, gated):
-    chans = out_ref.shape[1]
     d_pred, d_cross = factor_ref[:, 0, :], factor_ref[:, 1, :]
     for a in range(LAT_DEV):
         rows = slice(a * CP, (a + 1) * CP)
@@ -152,29 +188,42 @@
             g = target_ref[rows, cols].astype(jnp.float32)
             grads[rows, cols] = (lat_ref[a] * (2.0 * s * d_pred + g * d_cross)).astype(jnp.bfloat16)
     grid_grad = jnp.dot(grads[...], table_ref[...], preferred_element_type=jnp.float32)
+    gated[:ROWS, :] = grid_grad[:, :MAIN]
+    gated[ROWS:, :] = jnp.concatenate(
+        [grid_grad[a * CP : (a + 1) * CP, MAIN:LON] for a in range(LAT_DEV)], axis=1
+    )
     total[...] = jnp.zeros_like(total)
-    gated[...] = grid_grad
 
     def row(a, _):
-        for t in range(LONP // TILE):
+        for t in range(MAIN // TILE):
             cols = slice(t * TILE, (t + 1) * TILE)
             value = gated[pl.ds(pl.multiple_of(a * CP, CP), CP), cols]
             for m in range(J):
-                refs = cell_ref[m, pl.ds(a, 1), cols]
-                owner, hot = one_hot(refs)
+                owner, hot = one_hot(cell_ref[m, pl.ds(a, 1), cols])
+                shared = shared_owner(owner)
                 part = weight_ref[m, pl.ds(a, 1), cols] * value
-                spread = jnp.concatenate(
-                    [jnp.where(owner == o, part, 0.0).astype(jnp.bfloat16) for o in range(owners)],
-                    axis=0,
-                )
+                body, last = part[:BODY], part[BODY:]
+                first = lax.broadcasted_iota(jnp.int32, last.shape, 0) < HALF
+                half = jnp.where(first, last, pltpu.roll(last, HALF, 0))
+                pieces = []
+                for p in range(owners // 2):
+                    pieces.append(jnp.where(owner == 2 * p, body, 0.0))
+                    pieces.append(jnp.where(shared == p, half, 0.0))
+                    pieces.append(jnp.where(owner == 2 * p + 1, body, 0.0))
+                spread = jnp.concatenate(pieces, axis=0).astype(jnp.bfloat16)
                 total[...] += lax.dot_general(
                     spread, hot, (((1,), (1,)), ((), ())), preferred_element_type=jnp.float32
                 )
         return 0
 
-    lax.fori_loop(0, LAT_DEV, row, 0)
-    for o in range(owners):
-        out_ref[o] = total[o * CP : o * CP + chans, :].astype(jnp.bfloat16)
+    lax.fori_loop(0, CELL_ROWS, row, 0)
+    for p in range(owners // 2):
+        block = total[p * PAIR : (p + 1) * PAIR, :]
+        shared = block[BODY : BODY + 2 * HALF]
+        even = jnp.concatenate([block[:BODY], shared[:HALF]], axis=0)
+        odd = jnp.concatenate([block[BODY + 2 * HALF :], shared[HALF:]], axis=0)
+        out_ref[2 * p] = even.astype(jnp.bfloat16)
+        out_ref[2 * p + 1] = odd.astype(jnp.bfloat16)
 
 
 SMEM = pl.BlockSpec(memory_space=pltpu.SMEM)
@@ -188,7 +237,13 @@
 
 def everyone(block, axis):
     count = lax.axis_size(axis)
-    return exchange(jnp.broadcast_to(block[None], (count,) + block.shape), axis)
+    shifts = [[(i, (i + d) % count) for i in range(count)] for d in range(1, count)]
+    return [block] + [lax.ppermute(block, axis, shift) for shift in shifts]
+
+
+def cell_rows(cells):
+    rest = cells[:, :, MAIN:].reshape(J, 1, LAT_DEV * REST)
+    return jnp.concatenate([cells[:, :, :MAIN], rest], axis=1)
 
 
 def shards(node_values, block_slot, cell_ref, cell_weight, target_spectrum, spec_weight):
@@ -207,11 +262,11 @@
         compiler_params=PARAMS,
         name="pack",
     )(block_slot, node_values[0])
+    outgoing, target_spectrum = lax.optimization_barrier((outgoing, target_spectrum))
     received = exchange(outgoing, "band")
 
-    pad = ((0, 0), (0, 0), (0, LONP - LON))
-    refs = jnp.pad(cell_ref, pad, constant_values=-1)
-    weights = jnp.pad(cell_weight, pad)
+    refs = cell_rows(cell_ref)
+    weights = cell_rows(cell_weight)
     target = jnp.pad(
         jnp.transpose(target_spectrum[0].reshape(chans, LAT_DEV, 2 * K), (1, 0, 2)),
         ((0, 0), (0, CP - chans), (0, 0)),
@@ -236,15 +291,20 @@
             jax.ShapeDtypeStruct((ROWS, 2 * K), jnp.bfloat16),
             jax.ShapeDtypeStruct((CP, 4, K), jnp.float32),
         ),
-        in_specs=[SMEM] + [VMEM] * 7,
+        in_specs=[SMEM] + [VMEM] * 3 + [pl.BlockSpec(memory_space=pl.ANY)]
+        + [VMEM] * (2 + len(energies)),
         out_specs=(VMEM, VMEM),
         scratch_shapes=[
-            pltpu.VMEM((owners * CP, LO), jnp.bfloat16),
-            pltpu.VMEM((ROWS, LONP), jnp.bfloat16),
+            pltpu.VMEM((owners * CHANS, LO), jnp.float32),
+            pltpu.VMEM((owners * CHANS, LO), jnp.bfloat16),
+            pltpu.VMEM((CELL_ROWS * CP, MAIN), jnp.bfloat16),
+            pltpu.VMEM((ROWS, TILE), jnp.bfloat16),
+            pltpu.VMEM(table.shape, jnp.bfloat16),
+            pltpu.SemaphoreType.DMA,
         ],
         compiler_params=PARAMS,
         name="forward",
-    )(lat_weight, received, refs, weights, table, target, true_part, energies)
+    )(lat_weight, received, refs, weights, table, target, true_part, *energies)
 
     parts = exchange(sums, "band")
     factors = pl.pallas_call(
@@ -264,8 +324,8 @@
         out_specs=VMEM,
         scratch_shapes=[
             pltpu.VMEM((ROWS, 2 * K), jnp.bfloat16),
-            pltpu.VMEM((owners * CP, LO), jnp.float32),
-            pltpu.VMEM((ROWS, LONP), jnp.float32),
+            pltpu.VMEM((owners * CHANS, LO), jnp.float32),
+            pltpu.VMEM((CELL_ROWS * CP, MAIN), jnp.float32),
         ],
         compiler_params=PARAMS,
         name="backward",

time: 145 us -> 132 us (0.910)
  waiting for transfers between devices: 21.5 us -> 5.48 us
  Pallas kernels: 50.2 us -> 45.3 us
  blocking collectives: 51.1 us -> 54.8 us
  starting transfers between devices: 15.7 us -> 19.1 us
    all_to_all x2 -> x1, waiting for transfers between devices: 21.5 us -> 2.13 us  [exchange(): return lax.all_to_all(blocks, axis, split_axis=0, concat_axis=0, tiled=True)]
    ppermute x0 -> x7, starting transfers between devices: none -> 7.92 us  [everyone(): return [block] + [lax.ppermute(block, axis, shift) for shift in shifts]]
    all_to_all x2 -> x1, starting transfers between devices: 15.7 us -> 11.2 us  [exchange(): return lax.all_to_all(blocks, axis, split_axis=0, concat_axis=0, tiled=True)]
    all_to_all x3, blocking collectives: 51.1 us -> 54.8 us  [exchange(): return lax.all_to_all(blocks, axis, split_axis=0, concat_axis=0, tiled=True)]
    ppermute x0 -> x7, waiting for transfers between devices: none -> 3.35 us  [everyone(): return [block] + [lax.ppermute(block, axis, shift) for shift in shifts]]
    pallas_call x1, Pallas kernels: 23 us -> 19.9 us  [shards(): pl.pallas_call(functools.partial(backward_kernel, owners), out_shape=jax....]
    pallas_call x1, Pallas kernels: 23.4 us -> 21.6 us  [shards(): pl.pallas_call(functools.partial(forward_kernel, owners), out_shape=(jax....]
    unnamed x12 -> x10, local copies, waits for them, and re-layouts: 2.13 us -> 3.73 us
  transfers between devices with their start and end apart: 2 -> 8, of which waited for: 2 -> 4; matrix products, arithmetic and copies ran while one was open for 0% -> 2% of each run, Pallas kernels for 1% -> 1%
where the time goes in v3:
time: 132 us
  blocking collectives  54.8 us (42%)
  Pallas kernels  45.3 us (34%)
  starting transfers between devices  19.1 us (14%)
  local copies, waits for them, and re-layouts  6.83 us (5%)
  waiting for transfers between devices  5.48 us (4%)
    all_to_all x3, blocking collectives, exchange(): return lax.all_to_all(blocks, axis, split_axis=0, concat_axis=0, tiled=True)  54.8 us
    pallas_call x1, Pallas kernels, shards(): pl.pallas_call(functools.partial(forward_kernel, owners), out_shape=(jax....  21.6 us
    pallas_call x1, Pallas kernels, shards(): pl.pallas_call(functools.partial(backward_kernel, owners), out_shape=jax....  19.9 us
    all_to_all x1, starting transfers between devices, exchange(): return lax.all_to_all(blocks, axis, split_axis=0, concat_axis=0, tiled=True)  11.2 us
    ppermute x7, starting transfers between devices, everyone(): return [block] + [lax.ppermute(block, axis, shift) for shift in shifts]  7.92 us
    unnamed x10, local copies, waits for them, and re-layouts  3.73 us
    ppermute x7, waiting for transfers between devices, everyone(): return [block] + [lax.ppermute(block, axis, shift) for shift in shifts]  3.35 us
  transfers between devices with their start and end apart: 8, of which 4 were waited for; matrix products, arithmetic and copies ran while one was open for 2% of the time, Pallas kernels for 1%

profile of v3, /device:TPU:32, one launch (start us, length us, event | category | flops | bytes accessed | tf_op | source)
XLA Modules:
  0.0 131.8 jit_solution(6233709797483373096)
XLA Ops:
  0.0 0.0 copy-start.2
  0.0 0.9 copy-done.2
  1.0 0.0 copy-start.3
  1.0 0.7 copy-done.3
  1.6 0.0 slice-start.2
  1.6 0.0 slice-start.3
  1.6 0.0 slice-start
  1.6 0.0 slice-start.1
  1.6 1.4 %pack.1 = bf16[32,28,256]{2,1,0:T(8,128)(2,1)} custom-call(s32[32]{0:T(128)S(1)} %copy-done.3, bf16[28,4096]{1,0:T(8,128)(2,1)S(1)} %bitcast.9), custom_call_target="tpu_custom_call" | custom-call | tf_op jit(solution)/shard_map/pack/pallas_call | solution.py:257
  3.1 11.2 %all-to-all-start = ((bf16[32,28,256]{2,1,0:T(8,128)(2,1)}), bf16[32,28,256]{2,1,0:T(8,128)(2,1)S(1)}, u32[]{:S(2)}, u32[]{:S(2)}) async-start(bf16[32,28,256]{2,1,0:T(8,128)(2,1)} %pack.1), calls=%async_computation | async-start | bytes 1048576 | tf_op jit(solution)/shard_map/all_to_all | solution.py:235
  14.3 0.7 broadcast_in_dim.7.spec_weight_ref
  15.0 2.1 %reshape_squeeze.3 = bf16[28,8,1280]{2,1,0:T(8,128)(2,1)S(1)} reshape(bf16[1,28,8,2,640]{4,3,2,1,0:T(2,128)(2,1)} %param.11) | data formatting | bytes 1146880 | tf_op jit(solution)/shard_map/reshape;squeeze | solution.py:271
  17.0 0.1 copy.10
  17.3 0.9 true_power.1
  18.2 1.9 %collective-permute-start.6 = (f32[8,128]{1,0:T(8,128)S(1)}, f32[8,128]{1,0:T(8,128)S(1)}, u32[]{:S(2)}, u32[]{:S(2)}) collective-permute-start(f32[8,128]{1,0:T(8,128)S(1)} %get-tuple-element.14.refs_0_), channel_id=1, source_target_pairs={{0,7},{1,0},{2,1},{3,2},{4,3},{5,4},{6,5},{7,6},{8,15},{9,8},{10,9... | collective-permute-start | bytes 12296 | tf_op jit(solution)/shard_map/ppermute | solution.py:241
  20.1 1.2 collective-permute-start.5
  21.3 0.4 collective-permute-start.4
  21.7 2.9 %collective-permute-start.3 = (f32[8,128]{1,0:T(8,128)S(1)}, f32[8,128]{1,0:T(8,128)S(1)}, u32[]{:S(2)}, u32[]{:S(2)}) collective-permute-start(f32[8,128]{1,0:T(8,128)S(1)} %get-tuple-element.14.refs_0_), channel_id=1, source_target_pairs={{0,4},{1,5},{2,6},{3,7},{4,0},{5,1},{6,2},{7,3},{8,12},{9,13},{10,... | collective-permute-start | bytes 12296 | tf_op jit(solution)/shard_map/ppermute | solution.py:241
  24.6 0.0 collective-permute-start.2
  24.6 0.0 slice-done.2
  24.6 0.1 reshape.9
  24.7 0.0 slice-done.3
  24.7 0.0 slice-done
  24.7 0.1 reshape.10
  24.8 0.0 collective-permute-done.6.refs_7_
  24.8 0.5 collective-permute-start.1
  25.3 0.0 collective-permute-done.5.refs_6_
  25.3 1.1 collective-permute-start
  26.4 0.0 slice-done.1
  26.4 0.0 collective-permute-done.4.refs_5_
  26.4 0.4 collective-permute-done.3.refs_4_
  26.8 2.3 %collective-permute-done.2.refs_3_ = f32[8,128]{1,0:T(8,128)S(1)} collective-permute-done((f32[8,128]{1,0:T(8,128)S(1)}, f32[8,128]{1,0:T(8,128)S(1)}, u32[]{:S(2)}, u32[]{:S(2)}) %collective-permute-start.2) | collective-permute-done | bytes 4128 | tf_op jit(solution)/shard_map/ppermute | solution.py:241
  29.1 0.6 collective-permute-done.1.refs_2_
  29.7 0.0 collective-permute-done.refs_1_
  29.7 2.1 %all-to-all-done.buf_ref = bf16[32,28,256]{2,1,0:T(8,128)(2,1)S(1)} async-done(((bf16[32,28,256]{2,1,0:T(8,128)(2,1)}), bf16[32,28,256]{2,1,0:T(8,128)(2,1)S(1)}, u32[]{:S(2)}, u32[]{:S(2)}) %all-to-all-start) | async-done | bytes 458784 | tf_op jit(solution)/shard_map/all_to_all | solution.py:235
  31.9 0.0 copy-start
  31.9 2.1 %copy-done = bf16[1280,1536]{1,0:T(8,128)(2,1)S(1)} copy-done((bf16[1280,1536]{1,0:T(8,128)(2,1)S(1)}, bf16[1280,1536]{1,0:T(8,128)(2,1)}, u32[]{:S(2)}) %copy-start) | copy-done | bytes 3932184
  34.0 0.0 copy-start.1
  34.0 21.6 %forward.1 = (bf16[256,1280]{1,0:T(8,128)(2,1)S(1)}, f32[32,4,640]{2,1,0:T(4,128)S(1)}) custom-call(f32[8]{0:T(128)S(1)} %add_cosine_fusion.lat_ref, bf16[32,28,256]{2,1,0:T(8,128)(2,1)S(1)} %all-to-all-done.buf_ref, s32[3,9,1280]{2,1,0:T(8,128)S(1)} %pad_add_fusion.cell_ref, f32[3,9,1280]{2,1,0:T(8,128)S(1)} %pad_maximum_fusion.weight_ref, ...), custom_call_target="tpu_custom_call" | custom-call | tf_op jit(solution)/shard_map/forward/pallas_call | solution.py:288
  55.6 20.8 %all_to_all.20.parts_ref = f32[32,4,640]{2,1,0:T(4,128)S(1)} all-to-all(f32[32,4,640]{2,1,0:T(4,128)S(1)} %get-tuple-element.16), channel_id=1, replica_groups=mesh['band'=32,'chan'=8] {'band'}, dimensions={0} | all-to-all | bytes 655360 | tf_op jit(solution)/shard_map/all_to_all | solution.py:235
  76.4 0.1 middle.1
  76.5 0.0 copy-start.4
  76.5 14.5 %all_to_all.21.factor_ref = f32[32,2,640]{2,1,0:T(2,128)S(1)} all-to-all(f32[32,2,640]{2,1,0:T(2,128)S(1)} %middle.1), channel_id=1, replica_groups=mesh['band'=32,'chan'=8] {'band'}, dimensions={0} | all-to-all | bytes 327680 | tf_op jit(solution)/shard_map/all_to_all | solution.py:235
  91.0 0.0 copy-done.1
  91.0 19.9 %backward.1 = bf16[32,28,256]{2,1,0:T(8,128)(2,1)S(1)} custom-call(f32[8]{0:T(128)S(1)} %add_cosine_fusion.lat_ref, s32[3,9,1280]{2,1,0:T(8,128)S(1)} %pad_add_fusion.cell_ref, f32[3,9,1280]{2,1,0:T(8,128)S(1)} %pad_maximum_fusion.weight_ref, bf16[1280,1536]{1,0:T(8,128)(2,1)S(1)} %copy-done.1, bf16[256,1280]{1,0:T(8,128)(2,1)S(1)} %bitcast.8, ...), custom_call_target="tpu_custom_call" | custom-call | tf_op jit(solution)/shard_map/backward/pallas_call | solution.py:320
  110.9 19.5 %all_to_all.22.blocks_ref = bf16[32,28,256]{2,1,0:T(8,128)(2,1)S(1)} all-to-all(bf16[32,28,256]{2,1,0:T(8,128)(2,1)S(1)} %backward.1), channel_id=1, replica_groups=mesh['band'=32,'chan'=8] {'band'}, dimensions={0} | all-to-all | bytes 917504 | tf_op jit(solution)/shard_map/all_to_all | solution.py:235
  130.4 0.0 copy-done.4
  130.4 1.4 %unpack.1 = bf16[28,4096]{1,0:T(8,128)(2,1)} custom-call(s32[32]{0:T(128)S(1)} %copy-done.4, bf16[32,28,256]{2,1,0:T(8,128)(2,1)S(1)} %all_to_all.22.blocks_ref), custom_call_target="tpu_custom_call" | custom-call | tf_op jit(solution)/shard_map/unpack/pallas_call | solution.py:335
  (4 shorter events, 0.1 us)
Async XLA Ops:
  0.0 0.9 copy-start.2
  1.0 0.7 copy-start.3
  1.6 23.0 %slice-start.2 = ((s32[3,8,1440]{2,1,0:T(8,128)}), s32[3,8,160]{2,1,0:T(8,128)S(1)}, s32[]{:S(2)}) async-start(s32[3,8,1440]{2,1,0:T(8,128)} %param.9), calls=%async_computation.6 | async-start | bytes 49152 | tf_op jit(solution)/shard_map/slice | solution.py:245
  1.6 23.1 %slice-start.3 = ((s32[3,8,1440]{2,1,0:T(8,128)}), s32[3,8,1280]{2,1,0:T(8,128)S(1)}, s32[]{:S(2)}) async-start(s32[3,8,1440]{2,1,0:T(8,128)} %param.9), calls=%async_computation.7 | async-start | bytes 245760 | tf_op jit(solution)/shard_map/slice | solution.py:246
  1.6 23.1 %slice-start = ((f32[3,8,1440]{2,1,0:T(8,128)}), f32[3,8,160]{2,1,0:T(8,128)S(1)}, s32[]{:S(2)}) async-start(f32[3,8,1440]{2,1,0:T(8,128)} %param.10), calls=%async_computation.4 | async-start | bytes 49152 | tf_op jit(solution)/shard_map/slice | solution.py:245
  1.6 24.7 %slice-start.1 = ((f32[3,8,1440]{2,1,0:T(8,128)}), f32[3,8,1280]{2,1,0:T(8,128)S(1)}, s32[]{:S(2)}) async-start(f32[3,8,1440]{2,1,0:T(8,128)} %param.10), calls=%async_computation.5 | async-start | bytes 245760 | tf_op jit(solution)/shard_map/slice | solution.py:246
  3.1 28.8 %all-to-all-start = ((bf16[32,28,256]{2,1,0:T(8,128)(2,1)}), bf16[32,28,256]{2,1,0:T(8,128)(2,1)S(1)}, u32[]{:S(2)}, u32[]{:S(2)}) async-start(bf16[32,28,256]{2,1,0:T(8,128)(2,1)} %pack.1), calls=%async_computation | async-start | bytes 1048576 | tf_op jit(solution)/shard_map/all_to_all | solution.py:235
  18.2 6.7 %collective-permute-start.6 = (f32[8,128]{1,0:T(8,128)S(1)}, f32[8,128]{1,0:T(8,128)S(1)}, u32[]{:S(2)}, u32[]{:S(2)}) collective-permute-start(f32[8,128]{1,0:T(8,128)S(1)} %get-tuple-element.14.refs_0_), channel_id=1, source_target_pairs={{0,7},{1,0},{2,1},{3,2},{4,3},{5,4},{6,5},{7,6},{8,15},{9,8},{10,9... | collective-permute-start | bytes 12296 | tf_op jit(solution)/shard_map/ppermute | solution.py:241
  20.1 5.2 %collective-permute-start.5 = (f32[8,128]{1,0:T(8,128)S(1)}, f32[8,128]{1,0:T(8,128)S(1)}, u32[]{:S(2)}, u32[]{:S(2)}) collective-permute-start(f32[8,128]{1,0:T(8,128)S(1)} %get-tuple-element.14.refs_0_), channel_id=1, source_target_pairs={{0,6},{1,7},{2,0},{3,1},{4,2},{5,3},{6,4},{7,5},{8,14},{9,15},{10,... | collective-permute-start | bytes 12296 | tf_op jit(solution)/shard_map/ppermute | solution.py:241
  21.3 5.1 %collective-permute-start.4 = (f32[8,128]{1,0:T(8,128)S(1)}, f32[8,128]{1,0:T(8,128)S(1)}, u32[]{:S(2)}, u32[]{:S(2)}) collective-permute-start(f32[8,128]{1,0:T(8,128)S(1)} %get-tuple-element.14.refs_0_), channel_id=1, source_target_pairs={{0,5},{1,6},{2,7},{3,0},{4,1},{5,2},{6,3},{7,4},{8,13},{9,14},{10,... | collective-permute-start | bytes 12296 | tf_op jit(solution)/shard_map/ppermute | solution.py:241
  21.7 5.1 %collective-permute-start.3 = (f32[8,128]{1,0:T(8,128)S(1)}, f32[8,128]{1,0:T(8,128)S(1)}, u32[]{:S(2)}, u32[]{:S(2)}) collective-permute-start(f32[8,128]{1,0:T(8,128)S(1)} %get-tuple-element.14.refs_0_), channel_id=1, source_target_pairs={{0,4},{1,5},{2,6},{3,7},{4,0},{5,1},{6,2},{7,3},{8,12},{9,13},{10,... | collective-permute-start | bytes 12296 | tf_op jit(solution)/shard_map/ppermute | solution.py:241
  24.6 4.5 %collective-permute-start.2 = (f32[8,128]{1,0:T(8,128)S(1)}, f32[8,128]{1,0:T(8,128)S(1)}, u32[]{:S(2)}, u32[]{:S(2)}) collective-permute-start(f32[8,128]{1,0:T(8,128)S(1)} %get-tuple-element.14.refs_0_), channel_id=1, source_target_pairs={{0,3},{1,4},{2,5},{3,6},{4,7},{5,0},{6,1},{7,2},{8,11},{9,12},{10,... | collective-permute-start | bytes 12296 | tf_op jit(solution)/shard_map/ppermute | solution.py:241
  24.8 4.9 %collective-permute-start.1 = (f32[8,128]{1,0:T(8,128)S(1)}, f32[8,128]{1,0:T(8,128)S(1)}, u32[]{:S(2)}, u32[]{:S(2)}) collective-permute-start(f32[8,128]{1,0:T(8,128)S(1)} %get-tuple-element.14.refs_0_), channel_id=1, source_target_pairs={{0,2},{1,3},{2,4},{3,5},{4,6},{5,7},{6,0},{7,1},{8,10},{9,11},{10,... | collective-permute-start | bytes 12296 | tf_op jit(solution)/shard_map/ppermute | solution.py:241
  25.3 4.4 %collective-permute-start = (f32[8,128]{1,0:T(8,128)S(1)}, f32[8,128]{1,0:T(8,128)S(1)}, u32[]{:S(2)}, u32[]{:S(2)}) collective-permute-start(f32[8,128]{1,0:T(8,128)S(1)} %get-tuple-element.14.refs_0_), channel_id=1, source_target_pairs={{0,1},{1,2},{2,3},{3,4},{4,5},{5,6},{6,7},{7,0},{8,9},{9,10},{10,1... | collective-permute-start | bytes 12296 | tf_op jit(solution)/shard_map/ppermute | solution.py:241
  31.9 2.1 %copy-start = (bf16[1280,1536]{1,0:T(8,128)(2,1)S(1)}, bf16[1280,1536]{1,0:T(8,128)(2,1)}, u32[]{:S(2)}) copy-start(bf16[1280,1536]{1,0:T(8,128)(2,1)} %constant.20.clone.table_hbm.table_ref) | copy-start | bytes 11796484
  34.0 57.0 %copy-start.1 = (bf16[1280,1536]{1,0:T(8,128)(2,1)S(1)}, bf16[1280,1536]{1,0:T(8,128)(2,1)}, u32[]{:S(2)}) copy-start(bf16[1280,1536]{1,0:T(8,128)(2,1)} %constant.20.clone.table_hbm.table_ref) | copy-start | bytes 11796484
  76.5 53.9 %copy-start.4 = (s32[32]{0:T(128)S(1)}, s32[32]{0:T(128)}, u32[]{:S(2)}) copy-start(s32[32]{0:T(128)} %slot_ref.3) | copy-start | bytes 388

commit v4 on v3

--- a/solution.py
+++ b/solution.py
@@ -18,12 +18,15 @@
 NBLK_DEV = 32
 CAP = 2
 
-LONP = 1536
+HALF_LON = LON // 2
+HALF_PAD = 768
 TILE = 256
 LO = CAP * NB
 CP = 32
-MAIN = LON - LON % TILE
-REST = LON - MAIN
+HALF_MAIN = 640
+HALF_REST = HALF_LON - HALF_MAIN
+MAIN = 2 * HALF_MAIN
+REST = 2 * HALF_REST
 CELL_ROWS = LAT_DEV + 1
 CHANS = 28
 HALF = 4
@@ -41,8 +44,13 @@
     phase_angle = np.float32(2.0 * math.pi / LON) * phase_count.astype(np.float32)
     norm_factor = np.float32(1.0 / math.sqrt(LON))
     table = np.stack([np.cos(phase_angle) * norm_factor, -np.sin(phase_angle) * norm_factor])
-    table = table.astype(jnp.bfloat16).reshape(2 * K, LON)
-    return np.pad(table, ((0, 0), (0, LONP - LON)))
+    table = table.astype(jnp.bfloat16).reshape(2 * K, LON)[:, :HALF_LON]
+    return np.pad(table, ((0, 0), (0, HALF_PAD - HALF_LON)))
+
+
+def half_sign():
+    wavenumber = lax.broadcasted_iota(jnp.int32, (1, 2 * K), 1)
+    return jnp.where((wavenumber & 1) == 0, 1.0, -1.0)
 
 
 def lat_weights(first_row, row_count, lat_total):
@@ -79,8 +87,8 @@
 
 def middle_kernel(scale, parts_ref, spec_weight_ref, out_ref):
     sums = jnp.sum(parts_ref[...], axis=0)
-    pred_power, true_power, cross_sum = sums[0:1], sums[1:2], sums[2:3]
-    energy = sums[3:4] * scale + epsilon
+    pred_power, true_power, cross_sum = sums[:, :K], sums[:, K : 2 * K], sums[:, 2 * K : 3 * K]
+    energy = sums[:, 3 * K : 3 * K + 1] * scale + epsilon
     loss_scale = spec_weight_ref[...] / energy
     amp_pred = jnp.sqrt(pred_power + epsilon)
     amp_true = jnp.sqrt(true_power + epsilon)
@@ -94,7 +102,7 @@
         / (2.0 * amp_pred)
     )
     d_cross = -loss_scale * (amp_pred / amp_true + amp_true / amp_pred)
-    both = jnp.concatenate([d_pred, d_cross], axis=0)
+    both = jnp.concatenate([d_pred, d_cross], axis=1)
     out_ref[...] = jnp.broadcast_to(both[None], out_ref.shape)
 
 
@@ -111,12 +119,10 @@
     return jnp.where((owner & 1) == wanted, owner >> 1, -1)
 
 
-def forward_kernel(owners, lat_ref, buf_ref, cell_ref, weight_ref, table_hbm, target_ref,
-                   true_ref, *refs):
-    energy_refs = refs[:-8]
-    spec_ref, sums_ref, staged, nodes, grid, tail, table_ref, table_sem = refs[-8:]
-    table_copy = pltpu.make_async_copy(table_hbm, table_ref, table_sem)
-    table_copy.start()
+def gather_kernel(owners, buf_ref, cell_ref, weight_ref, *refs):
+    energy_refs = refs[:-5]
+    grid_ref, energy_ref, staged, nodes, grid = refs[-5:]
+    energy_ref[...] = sum((ref[...] for ref in energy_refs[1:]), energy_refs[0][...])
     for p in range(owners // 2):
         even = buf_ref[2 * p].astype(jnp.float32)
         odd = buf_ref[2 * p + 1].astype(jnp.float32)
@@ -148,17 +154,25 @@
 
     lax.fori_loop(0, CELL_ROWS, row, 0)
     rest = grid[ROWS : ROWS + CP, :].astype(jnp.float32)
-    for a in range(LAT_DEV):
-        piece = rest[:, a * REST : (a + 1) * REST]
-        piece = jnp.concatenate([piece, jnp.zeros((CP, TILE - REST), jnp.float32)], axis=1)
-        tail[a * CP : (a + 1) * CP, :] = piece.astype(jnp.bfloat16)
-    table_copy.wait()
-    contract = (((1,), (1,)), ((), ()))
-    spectrum = lax.dot_general(
-        grid[:ROWS, :], table_ref[:, :MAIN], contract, preferred_element_type=jnp.float32
-    ) + lax.dot_general(
-        tail[...], table_ref[:, MAIN:], contract, preferred_element_type=jnp.float32
+    zeros = jnp.zeros((CP, HALF_PAD - HALF_LON), jnp.float32)
+    for a in range(LAT_DEV):
+        for h in range(2):
+            at = a * REST + h * HALF_REST
+            piece = jnp.concatenate([rest[:, at : at + HALF_REST], zeros], axis=1)
+            rows = slice(h * ROWS + a * CP, h * ROWS + (a + 1) * CP)
+            grid_ref[rows, HALF_MAIN:] = piece.astype(jnp.bfloat16)
+    for h in range(2):
+        columns = slice(h * HALF_MAIN, (h + 1) * HALF_MAIN)
+        grid_ref[h * ROWS : (h + 1) * ROWS, :HALF_MAIN] = grid[:ROWS, columns]
+
+
+def spectrum_kernel(lat_ref, grid_ref, table_ref, target_ref, true_ref, energy_ref, spec_ref,
+                    sums_ref):
+    halves = lax.dot_general(
+        grid_ref[...], table_ref[...], (((1,), (1,)), ((), ())),
+        preferred_element_type=jnp.float32,
     )
+    spectrum = halves[:ROWS] + half_sign() * halves[ROWS:]
     spec_ref[...] = spectrum.astype(jnp.bfloat16)
     pred = jnp.zeros((CP, 2 * K), jnp.float32)
     cross = jnp.zeros((CP, 2 * K), jnp.float32)
@@ -168,30 +182,36 @@
         ws = lat_ref[a] * s
         pred = pred + ws * s
         cross = cross + ws * g
-    energy = energy_refs[0][0:1, 0:1]
-    for energy_ref in energy_refs[1:]:
-        energy = energy + energy_ref[0:1, 0:1]
-    sums_ref[:, 0, :] = pred[:, :K] + pred[:, K:]
-    sums_ref[:, 1, :] = true_ref[...]
-    sums_ref[:, 2, :] = cross[:, :K] + cross[:, K:]
-    sums_ref[:, 3, :] = jnp.broadcast_to(energy, (CP, K))
+    sums_ref[:, 0, :K] = pred[:, :K] + pred[:, K:]
+    sums_ref[:, 0, K : 2 * K] = true_ref[...]
+    sums_ref[:, 0, 2 * K : 3 * K] = cross[:, :K] + cross[:, K:]
+    sums_ref[:, 0, 3 * K :] = jnp.broadcast_to(energy_ref[0:1, :], (CP, NB))
 
 
 def backward_kernel(owners, lat_ref, cell_ref, weight_ref, table_ref, target_ref, spec_ref,
                     factor_ref, out_ref, grads, total, gated):
-    d_pred, d_cross = factor_ref[:, 0, :], factor_ref[:, 1, :]
+    d_pred, d_cross = factor_ref[:, 0, :K], factor_ref[:, 0, K:]
+    sign = half_sign()[:, :K]
     for a in range(LAT_DEV):
         rows = slice(a * CP, (a + 1) * CP)
         for r in range(2):
             cols = slice(r * K, (r + 1) * K)
             s = spec_ref[rows, cols].astype(jnp.float32)
             g = target_ref[rows, cols].astype(jnp.float32)
-            grads[rows, cols] = (lat_ref[a] * (2.0 * s * d_pred + g * d_cross)).astype(jnp.bfloat16)
+            grad = lat_ref[a] * (2.0 * s * d_pred + g * d_cross)
+            grads[rows, cols] = grad.astype(jnp.bfloat16)
+            flipped = slice(ROWS + a * CP, ROWS + (a + 1) * CP)
+            grads[flipped, cols] = (grad * sign).astype(jnp.bfloat16)
     grid_grad = jnp.dot(grads[...], table_ref[...], preferred_element_type=jnp.float32)
-    gated[:ROWS, :] = grid_grad[:, :MAIN]
-    gated[ROWS:, :] = jnp.concatenate(
-        [grid_grad[a * CP : (a + 1) * CP, MAIN:LON] for a in range(LAT_DEV)], axis=1
-    )
+    rest = []
+    for h in range(2):
+        columns = slice(h * HALF_MAIN, (h + 1) * HALF_MAIN)
+        gated[:ROWS, columns] = grid_grad[h * ROWS : (h + 1) * ROWS, :HALF_MAIN]
+    for a in range(LAT_DEV):
+        for h in range(2):
+            rows = slice(h * ROWS + a * CP, h * ROWS + (a + 1) * CP)
+            rest.append(grid_grad[rows, HALF_MAIN:HALF_LON])
+    gated[ROWS:, :] = jnp.concatenate(rest, axis=1)
     total[...] = jnp.zeros_like(total)
 
     def row(a, _):
@@ -228,7 +248,7 @@
 
 SMEM = pl.BlockSpec(memory_space=pltpu.SMEM)
 VMEM = pl.BlockSpec(memory_space=pltpu.VMEM)
-PARAMS = pltpu.CompilerParams(vmem_limit_bytes=40 * 1024 * 1024)
+PARAMS = pltpu.CompilerParams(vmem_limit_bytes=24 * 1024 * 1024)
 
 
 def exchange(blocks, axis):
@@ -237,13 +257,16 @@
 
 def everyone(block, axis):
     count = lax.axis_size(axis)
-    shifts = [[(i, (i + d) % count) for i in range(count)] for d in range(1, count)]
+    block = block + lax.ppermute(block, axis, [(i, i ^ 1) for i in range(count)])
+    shifts = [[(i, (i + d) % count) for i in range(count)] for d in range(2, count, 2)]
     return [block] + [lax.ppermute(block, axis, shift) for shift in shifts]
 
 
 def cell_rows(cells):
-    rest = cells[:, :, MAIN:].reshape(J, 1, LAT_DEV * REST)
-    return jnp.concatenate([cells[:, :, :MAIN], rest], axis=1)
+    first, second = cells[:, :, :HALF_LON], cells[:, :, HALF_LON:]
+    rest = jnp.concatenate([first[:, :, HALF_MAIN:], second[:, :, HALF_MAIN:]], axis=2)
+    main = jnp.concatenate([first[:, :, :HALF_MAIN], second[:, :, :HALF_MAIN]], axis=2)
+    return jnp.concatenate([main, rest.reshape(J, 1, LAT_DEV * REST)], axis=1)
 
 
 def shards(node_values, block_slot, cell_ref, cell_weight, target_spectrum, spec_weight):
@@ -259,10 +282,12 @@
         out_shape=jax.ShapeDtypeStruct((owners, chans, LO), jnp.bfloat16),
         in_specs=[SMEM, VMEM],
         out_specs=VMEM,
-        compiler_params=PARAMS,
+        compiler_params=pltpu.CompilerParams(vmem_limit_bytes=60 * 1024 * 1024),
         name="pack",
     )(block_slot, node_values[0])
-    outgoing, target_spectrum = lax.optimization_barrier((outgoing, target_spectrum))
+    outgoing, target_spectrum, cell_ref, cell_weight, spec_weight = lax.optimization_barrier(
+        (outgoing, target_spectrum, cell_ref, cell_weight, spec_weight)
+    )
     received = exchange(outgoing, "band")
 
     refs = cell_rows(cell_ref)
@@ -285,31 +310,39 @@
     )(lat_weight, spec_weight[None, :], target)
     energies = everyone(energy_part, "chan")
 
-    spectrum, sums = pl.pallas_call(
-        functools.partial(forward_kernel, owners),
+    grid, energy = pl.pallas_call(
+        functools.partial(gather_kernel, owners),
         out_shape=(
-            jax.ShapeDtypeStruct((ROWS, 2 * K), jnp.bfloat16),
-            jax.ShapeDtypeStruct((CP, 4, K), jnp.float32),
+            jax.ShapeDtypeStruct((2 * ROWS, HALF_PAD), jnp.bfloat16),
+            jax.ShapeDtypeStruct(energy_part.shape, jnp.float32),
         ),
-        in_specs=[SMEM] + [VMEM] * 3 + [pl.BlockSpec(memory_space=pl.ANY)]
-        + [VMEM] * (2 + len(energies)),
+        in_specs=[VMEM] * (3 + len(energies)),
         out_specs=(VMEM, VMEM),
         scratch_shapes=[
             pltpu.VMEM((owners * CHANS, LO), jnp.float32),
             pltpu.VMEM((owners * CHANS, LO), jnp.bfloat16),
             pltpu.VMEM((CELL_ROWS * CP, MAIN), jnp.bfloat16),
-            pltpu.VMEM((ROWS, TILE), jnp.bfloat16),
-            pltpu.VMEM(table.shape, jnp.bfloat16),
-            pltpu.SemaphoreType.DMA,
         ],
         compiler_params=PARAMS,
-        name="forward",
-    )(lat_weight, received, refs, weights, table, target, true_part, *energies)
+        name="gather",
+    )(received, refs, weights, *energies)
+
+    spectrum, sums = pl.pallas_call(
+        spectrum_kernel,
+        out_shape=(
+            jax.ShapeDtypeStruct((ROWS, 2 * K), jnp.bfloat16),
+            jax.ShapeDtypeStruct((CP, 1, 3 * K + NB), jnp.float32),
+        ),
+        in_specs=[SMEM] + [VMEM] * 5,
+        out_specs=(VMEM, VMEM),
+        compiler_params=PARAMS,
+        name="spectrum",
+    )(lat_weight, grid, table, target, true_part, energy)
 
     parts = exchange(sums, "band")
     factors = pl.pallas_call(
         functools.partial(middle_kernel, 1.0 / (C * K * lat_total)),
-        out_shape=jax.ShapeDtypeStruct((owners, 2, K), jnp.float32),
+        out_shape=jax.ShapeDtypeStruct((owners, 1, 2 * K), jnp.float32),
         in_specs=[VMEM, VMEM],
         out_specs=VMEM,
         compiler_params=PARAMS,
@@ -323,7 +356,7 @@
         in_specs=[SMEM] + [VMEM] * 6,
         out_specs=VMEM,
         scratch_shapes=[
-            pltpu.VMEM((ROWS, 2 * K), jnp.bfloat16),
+            pltpu.VMEM((2 * ROWS, 2 * K), jnp.bfloat16),
             pltpu.VMEM((owners * CHANS, LO), jnp.float32),
             pltpu.VMEM((CELL_ROWS * CP, MAIN), jnp.float32),
         ],

time: 132 us -> 126 us (0.955)
  local copies, waits for them, and re-layouts: 6.83 us -> 1.72 us
  waiting for transfers between devices: 5.48 us -> 9.96 us
  blocking collectives: 54.8 us -> 50.4 us
  starting transfers between devices: 19.1 us -> 15.9 us
  Pallas kernels: 45.3 us -> 46.9 us
    all_to_all x3, blocking collectives: 54.8 us -> 50.4 us  [exchange(): return lax.all_to_all(blocks, axis, split_axis=0, concat_axis=0, tiled=True)]
    unnamed x10, local copies, waits for them, and re-layouts: 3.73 us -> 0.02 us
    all_to_all x1, waiting for transfers between devices: 2.13 us -> 5.71 us  [exchange(): return lax.all_to_all(blocks, axis, split_axis=0, concat_axis=0, tiled=True)]
    ppermute x7 -> x3, starting transfers between devices: 7.92 us -> 4.61 us  [everyone(): return [block] + [lax.ppermute(block, axis, shift) for shift in shifts]]
    another operation x2, local copies, waits for them, and re-layouts: 2.18 us -> 0.46 us  [shards(): target_spectrum[0].reshape(chans, LAT_DEV, 2 * K)]
    pallas_call x1 -> x2, Pallas kernels: 21.6 us -> 22.5 us  [the longest x1 20.5 us: shards(): pl.pallas_call(functools.partial(gather_kernel, owners), out_shape=(jax.S...]
    ppermute x7 -> x3, waiting for transfers between devices: 3.35 us -> 3.81 us  [everyone(): return [block] + [lax.ppermute(block, axis, shift) for shift in shifts]]
  transfers between devices with their start and end apart: 8 -> 5, of which waited for: 4 -> 4; matrix products, arithmetic and copies ran while one was open for 2% -> 2% of each run, Pallas kernels for 1% -> 1%
where the time goes in v4:
time: 126 us; the launch traced here: 125 us
  blocking collectives  50.4 us (40%)
  Pallas kernels  46.9 us (37%)
  starting transfers between devices  15.9 us (13%)
  waiting for transfers between devices  9.96 us (8%)
  local copies, waits for them, and re-layouts  1.72 us (1%)
    all_to_all x3, blocking collectives, exchange(): return lax.all_to_all(blocks, axis, split_axis=0, concat_axis=0, tiled=True)  50.4 us
    pallas_call x1, Pallas kernels, shards(): pl.pallas_call(functools.partial(gather_kernel, owners), out_shape=(jax.S...  20.5 us
    pallas_call x1, Pallas kernels, shards(): pl.pallas_call(functools.partial(backward_kernel, owners), out_shape=jax....  20 us
    all_to_all x1, starting transfers between devices, exchange(): return lax.all_to_all(blocks, axis, split_axis=0, concat_axis=0, tiled=True)  11.2 us
    all_to_all x1, waiting for transfers between devices, exchange(): return lax.all_to_all(blocks, axis, split_axis=0, concat_axis=0, tiled=True)  5.71 us
    ppermute x3, starting transfers between devices, everyone(): return [block] + [lax.ppermute(block, axis, shift) for shift in shifts]  4.61 us
    ppermute x3, waiting for transfers between devices, everyone(): return [block] + [lax.ppermute(block, axis, shift) for shift in shifts]  3.81 us
  transfers between devices with their start and end apart: 5, of which 4 were waited for; matrix products, arithmetic and copies ran while one was open for 2% of the time, Pallas kernels for 1%

profile of v4, /device:TPU:32, one launch (start us, length us, event | category | flops | bytes accessed | tf_op | source)
XLA Modules:
  0.0 125.4 jit_solution(8990514338780627924)
XLA Ops:
  0.0 0.0 copy-start.2
  0.0 1.9 %pack.1 = bf16[32,28,256]{2,1,0:T(8,128)(2,1)} custom-call(s32[32]{0:T(128)} %slot_ref.3, bf16[28,4096]{1,0:T(8,128)(2,1)} %bitcast.10), custom_call_target="tpu_custom_call" | custom-call | tf_op jit(solution)/shard_map/pack/pallas_call | solution.py:280
  1.9 11.2 %all-to-all-start = ((bf16[32,28,256]{2,1,0:T(8,128)(2,1)}), bf16[32,28,256]{2,1,0:T(8,128)(2,1)}, u32[]{:S(2)}, u32[]{:S(2)}) async-start(bf16[32,28,256]{2,1,0:T(8,128)(2,1)} %pack.1), calls=%async_computation | async-start | bytes 1048576 | tf_op jit(solution)/shard_map/all_to_all | solution.py:255
  13.2 0.7 broadcast_in_dim.7.spec_weight_ref
  13.9 0.0 copy-done.2
  13.9 0.0 copy-start.3
  13.9 0.4 reshape_squeeze.3
  14.3 0.0 copy-start.4
  14.3 0.1 copy.10
  14.4 0.0 copy-start
  14.5 0.9 true_power.1
  15.4 0.1 collective-permute-start
  15.5 0.0 copy-done.3
  15.5 0.1 fusion.3
  15.6 0.1 fusion.2
  15.7 0.0 copy-done.4
  15.7 0.1 fusion.1
  15.8 0.1 pad_add_fusion.1
  15.8 0.1 reshape.9
  15.9 0.1 fusion
  16.0 0.1 pad_maximum_fusion.1
  16.1 0.1 reshape.10
  16.2 0.4 collective-permute-done
  16.7 3.0 %collective-permute-start.3 = (f32[8,128]{1,0:T(8,128)S(1)}, f32[8,128]{1,0:T(8,128)S(1)}, u32[]{:S(2)}, u32[]{:S(2)}) collective-permute-start(f32[8,128]{1,0:T(8,128)S(1)} %add.18.refs_0_), channel_id=1, source_target_pairs={{0,6},{1,7},{2,0},{3,1},{4,2},{5,3},{6,4},{7,5},{8,14},{9,15},{10,... | collective-permute-start | bytes 12296 | tf_op jit(solution)/shard_map/ppermute | solution.py:262
  19.7 0.6 collective-permute-start.2
  20.3 1.0 collective-permute-start.1
  21.3 0.0 collective-permute-done.3.refs_3_
  21.3 3.5 %collective-permute-done.2.refs_2_ = f32[8,128]{1,0:T(8,128)S(1)} collective-permute-done((f32[8,128]{1,0:T(8,128)S(1)}, f32[8,128]{1,0:T(8,128)S(1)}, u32[]{:S(2)}, u32[]{:S(2)}) %collective-permute-start.2) | collective-permute-done | bytes 4128 | tf_op jit(solution)/shard_map/ppermute | solution.py:262
  24.8 0.3 collective-permute-done.1.refs_1_
  25.1 5.7 %all-to-all-done.buf_ref = bf16[32,28,256]{2,1,0:T(8,128)(2,1)} async-done(((bf16[32,28,256]{2,1,0:T(8,128)(2,1)}), bf16[32,28,256]{2,1,0:T(8,128)(2,1)}, u32[]{:S(2)}, u32[]{:S(2)}) %all-to-all-start) | async-done | bytes 458784 | tf_op jit(solution)/shard_map/all_to_all | solution.py:255
  30.8 20.5 %gather.1 = (bf16[512,768]{1,0:T(8,128)(2,1)S(1)}, f32[8,128]{1,0:T(8,128)S(1)}) custom-call(bf16[32,28,256]{2,1,0:T(8,128)(2,1)} %all-to-all-done.buf_ref, s32[3,9,1280]{2,1,0:T(8,128)S(1)} %pad_add_fusion.cell_ref, f32[3,9,1280]{2,1,0:T(8,128)S(1)} %pad_maximum_fusion.weight_ref, f32[8,128]{1,0:T(8,128)S(1)} %add.18.refs_0_, ...), custom_call_target="tpu_custom_call" | custom-call | tf_op jit(solution)/shard_map/gather/pallas_call | solution.py:313
  51.3 0.0 copy-done
  51.3 2.0 %spectrum.1 = (bf16[256,1280]{1,0:T(8,128)(2,1)S(1)}, f32[32,1,2048]{2,1,0:T(1,128)S(1)}) custom-call(f32[8]{0:T(128)S(1)} %add_cosine_fusion.lat_ref, bf16[512,768]{1,0:T(8,128)(2,1)S(1)} %get-tuple-element.22.grid_ref, bf16[1280,768]{1,0:T(8,128)(2,1)S(1)} %copy-done, bf16[256,1280]{1,0:T(8,128)(2,1)S(1)} %bitcast.7, ...), custom_call_target="tpu_custom_call" | custom-call | tf_op jit(solution)/shard_map/spectrum/pallas_call | solution.py:330
  53.3 16.3 %all_to_all.20.parts_ref = f32[32,1,2048]{2,1,0:T(1,128)S(1)} all-to-all(f32[32,1,2048]{2,1,0:T(1,128)S(1)} %get-tuple-element.26), channel_id=1, replica_groups=mesh['band'=32,'chan'=8] {'band'}, dimensions={0} | all-to-all | bytes 524288 | tf_op jit(solution)/shard_map/all_to_all | solution.py:255
  69.6 0.2 middle.1
  69.8 14.3 %all_to_all.21.factor_ref = f32[32,1,1280]{2,1,0:T(1,128)S(1)} all-to-all(f32[32,1,1280]{2,1,0:T(1,128)S(1)} %middle.1), channel_id=1, replica_groups=mesh['band'=32,'chan'=8] {'band'}, dimensions={0} | all-to-all | bytes 327680 | tf_op jit(solution)/shard_map/all_to_all | solution.py:255
  84.1 0.0 copy-start.1
  84.1 20.0 %backward.1 = bf16[32,28,256]{2,1,0:T(8,128)(2,1)S(1)} custom-call(f32[8]{0:T(128)S(1)} %add_cosine_fusion.lat_ref, s32[3,9,1280]{2,1,0:T(8,128)S(1)} %pad_add_fusion.cell_ref, f32[3,9,1280]{2,1,0:T(8,128)S(1)} %pad_maximum_fusion.weight_ref, bf16[1280,768]{1,0:T(8,128)(2,1)S(1)} %copy-done, bf16[256,1280]{1,0:T(8,128)(2,1)S(1)} %bitcast.8, ...), custom_call_target="tpu_custom_call" | custom-call | tf_op jit(solution)/shard_map/backward/pallas_call | solution.py:353
  104.2 19.9 %all_to_all.22.blocks_ref = bf16[32,28,256]{2,1,0:T(8,128)(2,1)S(1)} all-to-all(bf16[32,28,256]{2,1,0:T(8,128)(2,1)S(1)} %backward.1), channel_id=1, replica_groups=mesh['band'=32,'chan'=8] {'band'}, dimensions={0} | all-to-all | bytes 917504 | tf_op jit(solution)/shard_map/all_to_all | solution.py:255
  124.0 0.0 copy-done.1
  124.0 1.4 %unpack.1 = bf16[28,4096]{1,0:T(8,128)(2,1)} custom-call(s32[32]{0:T(128)S(1)} %copy-done.1, bf16[32,28,256]{2,1,0:T(8,128)(2,1)S(1)} %all_to_all.22.blocks_ref), custom_call_target="tpu_custom_call" | custom-call | tf_op jit(solution)/shard_map/unpack/pallas_call | solution.py:368
  (5 shorter events, 0.1 us)
Async XLA Ops:
  0.0 13.9 %copy-start.2 = (bf16[1,28,8,2,640]{4,3,2,1,0:T(2,128)(2,1)S(1)}, bf16[1,28,8,2,640]{4,3,2,1,0:T(2,128)(2,1)}, u32[]{:S(2)}) copy-start(bf16[1,28,8,2,640]{4,3,2,1,0:T(2,128)(2,1)} %param.11) | copy-start | bytes 1720324
  1.9 28.9 %all-to-all-start = ((bf16[32,28,256]{2,1,0:T(8,128)(2,1)}), bf16[32,28,256]{2,1,0:T(8,128)(2,1)}, u32[]{:S(2)}, u32[]{:S(2)}) async-start(bf16[32,28,256]{2,1,0:T(8,128)(2,1)} %pack.1), calls=%async_computation | async-start | bytes 1048576 | tf_op jit(solution)/shard_map/all_to_all | solution.py:255
  13.9 1.6 %copy-start.3 = (s32[3,8,1440]{2,1,0:T(8,128)S(1)}, s32[3,8,1440]{2,1,0:T(8,128)}, u32[]{:S(2)}) copy-start(s32[3,8,1440]{2,1,0:T(8,128)} %param.9) | copy-start | bytes 414724
  14.3 1.4 %copy-start.4 = (f32[3,8,1440]{2,1,0:T(8,128)S(1)}, f32[3,8,1440]{2,1,0:T(8,128)}, u32[]{:S(2)}) copy-start(f32[3,8,1440]{2,1,0:T(8,128)} %param.10) | copy-start | bytes 414724
  14.4 36.9 %copy-start = (bf16[1280,768]{1,0:T(8,128)(2,1)S(1)}, bf16[1280,768]{1,0:T(8,128)(2,1)}, u32[]{:S(2)}) copy-start(bf16[1280,768]{1,0:T(8,128)(2,1)} %constant.20.clone.table_ref) | copy-start | bytes 5898244
  15.4 1.3 collective-permute-start
  16.7 4.6 %collective-permute-start.3 = (f32[8,128]{1,0:T(8,128)S(1)}, f32[8,128]{1,0:T(8,128)S(1)}, u32[]{:S(2)}, u32[]{:S(2)}) collective-permute-start(f32[8,128]{1,0:T(8,128)S(1)} %add.18.refs_0_), channel_id=1, source_target_pairs={{0,6},{1,7},{2,0},{3,1},{4,2},{5,3},{6,4},{7,5},{8,14},{9,15},{10,... | collective-permute-start | bytes 12296 | tf_op jit(solution)/shard_map/ppermute | solution.py:262
  19.7 5.1 %collective-permute-start.2 = (f32[8,128]{1,0:T(8,128)S(1)}, f32[8,128]{1,0:T(8,128)S(1)}, u32[]{:S(2)}, u32[]{:S(2)}) collective-permute-start(f32[8,128]{1,0:T(8,128)S(1)} %add.18.refs_0_), channel_id=1, source_target_pairs={{0,4},{1,5},{2,6},{3,7},{4,0},{5,1},{6,2},{7,3},{8,12},{9,13},{10,... | collective-permute-start | bytes 12296 | tf_op jit(solution)/shard_map/ppermute | solution.py:262
  20.3 4.8 %collective-permute-start.1 = (f32[8,128]{1,0:T(8,128)S(1)}, f32[8,128]{1,0:T(8,128)S(1)}, u32[]{:S(2)}, u32[]{:S(2)}) collective-permute-start(f32[8,128]{1,0:T(8,128)S(1)} %add.18.refs_0_), channel_id=1, source_target_pairs={{0,2},{1,3},{2,4},{3,5},{4,6},{5,7},{6,0},{7,1},{8,10},{9,11},{10,... | collective-permute-start | bytes 12296 | tf_op jit(solution)/shard_map/ppermute | solution.py:262
  84.1 39.9 %copy-start.1 = (s32[32]{0:T(128)S(1)}, s32[32]{0:T(128)}, u32[]{:S(2)}) copy-start(s32[32]{0:T(128)} %slot_ref.3) | copy-start | bytes 388

commit v5 on v4

--- a/solution.py
+++ b/solution.py
@@ -59,19 +59,34 @@
     return jnp.cos(latitude)
 
 
-def pack_kernel(slot_ref, nodes_ref, out_ref):
-    out_ref[...] = jnp.zeros_like(out_ref)
+def first_rows(lanes):
+    return lax.broadcasted_iota(jnp.int32, (2 * HALF, lanes), 0) < HALF
+
+
+def pack_kernel(slot_ref, nodes_ref, out_ref, staged):
+    staged[...] = jnp.zeros_like(staged)
+    first = first_rows(NB)
     for i in range(NBLK_DEV):
-        slot = slot_ref[i]
-        half = pl.ds(pl.multiple_of((slot & 1) * NB, NB), NB)
-        out_ref[slot >> 1, :, half] = nodes_ref[:, i * NB : (i + 1) * NB]
-
-
-def unpack_kernel(slot_ref, blocks_ref, out_ref):
+        owner, slot = slot_ref[i] >> 1, slot_ref[i] & 1
+        block = nodes_ref[:, i * NB : (i + 1) * NB].astype(jnp.float32)
+        at = pl.multiple_of(slot * (BODY + 2 * HALF), 8)
+        staged[owner, pl.ds(at, BODY), :] = block[:BODY]
+        last = jnp.concatenate([block[BODY:], block[BODY:]], axis=0)
+        shared = staged[owner, BODY : BODY + 2 * HALF, :]
+        staged[owner, BODY : BODY + 2 * HALF, :] = jnp.where(first == (slot == 0), last, shared)
+    out_ref[...] = staged[...].astype(jnp.bfloat16)
+
+
+def unpack_kernel(slot_ref, blocks_ref, out_ref, staged):
+    staged[...] = blocks_ref[...].astype(jnp.float32)
     for i in range(NBLK_DEV):
-        slot = slot_ref[i]
-        half = pl.ds(pl.multiple_of((slot & 1) * NB, NB), NB)
-        out_ref[:, i * NB : (i + 1) * NB] = blocks_ref[slot >> 1, :, half]
+        owner, slot = slot_ref[i] >> 1, slot_ref[i] & 1
+        at = pl.multiple_of(slot * (BODY + 2 * HALF), 8)
+        body = staged[owner, pl.ds(at, BODY), :]
+        shared = staged[owner, BODY : BODY + 2 * HALF, :]
+        last = jnp.where(slot == 0, shared, pltpu.roll(shared, HALF, 0))[:HALF]
+        block = jnp.concatenate([body, last], axis=0)
+        out_ref[:, i * NB : (i + 1) * NB] = block.astype(jnp.bfloat16)
 
 
 def true_kernel(lat_ref, spec_weight_ref, target_ref, true_ref, energy_ref):
@@ -123,13 +138,22 @@
     energy_refs = refs[:-5]
     grid_ref, energy_ref, staged, nodes, grid = refs[-5:]
     energy_ref[...] = sum((ref[...] for ref in energy_refs[1:]), energy_refs[0][...])
+    first = first_rows(NB)
     for p in range(owners // 2):
         even = buf_ref[2 * p].astype(jnp.float32)
         odd = buf_ref[2 * p + 1].astype(jnp.float32)
-        staged[p * PAIR : p * PAIR + BODY, :] = even[:BODY]
-        shared = jnp.concatenate([even[BODY:], odd[BODY:]], axis=0)
-        staged[p * PAIR + BODY : p * PAIR + BODY + 2 * HALF, :] = shared
-        staged[p * PAIR + BODY + 2 * HALF : (p + 1) * PAIR, :] = odd[:BODY]
+        middle = slice(BODY, BODY + 2 * HALF)
+        tail = slice(BODY + 2 * HALF, PAIR)
+        at = p * PAIR
+        staged[at : at + BODY, :NB], staged[at : at + BODY, NB:] = even[:BODY], even[tail]
+        staged[at + BODY : at + BODY + 2 * HALF, :NB] = jnp.where(
+            first, even[middle], pltpu.roll(odd[middle], HALF, 0)
+        )
+        staged[at + BODY : at + BODY + 2 * HALF, NB:] = jnp.where(
+            first, pltpu.roll(even[middle], HALF, 0), odd[middle]
+        )
+        staged[at + BODY + 2 * HALF : at + PAIR, :NB] = odd[:BODY]
+        staged[at + BODY + 2 * HALF : at + PAIR, NB:] = odd[tail]
     nodes[...] = staged[...].astype(jnp.bfloat16)
 
     def row(a, _):
@@ -237,13 +261,20 @@
         return 0
 
     lax.fori_loop(0, CELL_ROWS, row, 0)
+    first = first_rows(NB)
     for p in range(owners // 2):
         block = total[p * PAIR : (p + 1) * PAIR, :]
-        shared = block[BODY : BODY + 2 * HALF]
-        even = jnp.concatenate([block[:BODY], shared[:HALF]], axis=0)
-        odd = jnp.concatenate([block[BODY + 2 * HALF :], shared[HALF:]], axis=0)
-        out_ref[2 * p] = even.astype(jnp.bfloat16)
-        out_ref[2 * p + 1] = odd.astype(jnp.bfloat16)
+        left, right = block[BODY : BODY + 2 * HALF, :NB], block[BODY : BODY + 2 * HALF, NB:]
+        even = jnp.where(first, left, pltpu.roll(right, HALF, 0))
+        odd = jnp.where(first, pltpu.roll(left, HALF, 0), right)
+        body = block[:BODY]
+        out_ref[2 * p] = jnp.concatenate([body[:, :NB], even, body[:, NB:]], axis=0).astype(
+            jnp.bfloat16
+        )
+        body = block[BODY + 2 * HALF :]
+        out_ref[2 * p + 1] = jnp.concatenate([body[:, :NB], odd, body[:, NB:]], axis=0).astype(
+            jnp.bfloat16
+        )
 
 
 SMEM = pl.BlockSpec(memory_space=pltpu.SMEM)
@@ -279,9 +310,10 @@
 
     outgoing = pl.pallas_call(
         pack_kernel,
-        out_shape=jax.ShapeDtypeStruct((owners, chans, LO), jnp.bfloat16),
+        out_shape=jax.ShapeDtypeStruct((owners, PAIR, NB), jnp.bfloat16),
         in_specs=[SMEM, VMEM],
         out_specs=VMEM,
+        scratch_shapes=[pltpu.VMEM((owners, PAIR, NB), jnp.float32)],
         compiler_params=pltpu.CompilerParams(vmem_limit_bytes=60 * 1024 * 1024),
         name="pack",
     )(block_slot, node_values[0])
@@ -352,7 +384,7 @@
 
     slot_grad = pl.pallas_call(
         functools.partial(backward_kernel, owners),
-        out_shape=jax.ShapeDtypeStruct((owners, chans, LO), jnp.bfloat16),
+        out_shape=jax.ShapeDtypeStruct((owners, PAIR, NB), jnp.bfloat16),
         in_specs=[SMEM] + [VMEM] * 6,
         out_specs=VMEM,
         scratch_shapes=[
@@ -370,6 +402,7 @@
         out_shape=jax.ShapeDtypeStruct((chans, nodes_local), jnp.bfloat16),
         in_specs=[SMEM, VMEM],
         out_specs=VMEM,
+        scratch_shapes=[pltpu.VMEM((owners, PAIR, NB), jnp.float32)],
         compiler_params=PARAMS,
         name="unpack",
     )(block_slot, returned)

time: 126 us -> 123 us (0.976)
  blocking collectives: 50.4 us -> 48.9 us
  waiting for transfers between devices: 9.96 us -> 8.56 us
    all_to_all x3, blocking collectives: 50.4 us -> 48.9 us  [exchange(): return lax.all_to_all(blocks, axis, split_axis=0, concat_axis=0, tiled=True)]
    all_to_all x1, waiting for transfers between devices: 5.71 us -> 4.3 us  [exchange(): return lax.all_to_all(blocks, axis, split_axis=0, concat_axis=0, tiled=True)]
where the time goes in v5:
time: 123 us
  blocking collectives  48.9 us (40%)
  Pallas kernels  47 us (38%)
  starting transfers between devices  15.9 us (13%)
  waiting for transfers between devices  8.56 us (7%)
  local copies, waits for them, and re-layouts  1.72 us (1%)
    all_to_all x3, blocking collectives, exchange(): return lax.all_to_all(blocks, axis, split_axis=0, concat_axis=0, tiled=True)  48.9 us
    pallas_call x1, Pallas kernels, shards(): pl.pallas_call(functools.partial(gather_kernel, owners), out_shape=(jax.S...  20.4 us
    pallas_call x1, Pallas kernels, shards(): pl.pallas_call(functools.partial(backward_kernel, owners), out_shape=jax....  20 us
    all_to_all x1, starting transfers between devices, exchange(): return lax.all_to_all(blocks, axis, split_axis=0, concat_axis=0, tiled=True)  11.2 us
    ppermute x3, starting transfers between devices, everyone(): return [block] + [lax.ppermute(block, axis, shift) for shift in shifts]  4.61 us
    all_to_all x1, waiting for transfers between devices, exchange(): return lax.all_to_all(blocks, axis, split_axis=0, concat_axis=0, tiled=True)  4.3 us
    ppermute x3, waiting for transfers between devices, everyone(): return [block] + [lax.ppermute(block, axis, shift) for shift in shifts]  3.81 us
  transfers between devices with their start and end apart: 5, of which 4 were waited for; matrix products, arithmetic and copies ran while one was open for 2% of the time, Pallas kernels for 1%

profile of v5, /device:TPU:32, one launch (start us, length us, event | category | flops | bytes accessed | tf_op | source)
XLA Modules:
  0.0 122.6 jit_solution(17320890401067135365)
XLA Ops:
  0.0 0.0 copy-start.2
  0.0 2.0 %pack.1 = bf16[32,56,128]{2,1,0:T(8,128)(2,1)} custom-call(s32[32]{0:T(128)} %slot_ref.3, bf16[28,4096]{1,0:T(8,128)(2,1)} %bitcast.10), custom_call_target="tpu_custom_call" | custom-call | tf_op jit(solution)/shard_map/pack/pallas_call | solution.py:311
  2.0 11.2 %all-to-all-start = ((bf16[32,56,128]{2,1,0:T(8,128)(2,1)}), bf16[32,56,128]{2,1,0:T(8,128)(2,1)}, u32[]{:S(2)}, u32[]{:S(2)}) async-start(bf16[32,56,128]{2,1,0:T(8,128)(2,1)} %pack.1), calls=%async_computation | async-start | bytes 917504 | tf_op jit(solution)/shard_map/all_to_all | solution.py:286
  13.3 0.7 broadcast_in_dim.7.spec_weight_ref
  14.0 0.0 copy-done.2
  14.0 0.0 copy-start.3
  14.0 0.4 reshape_squeeze.3
  14.4 0.0 copy-start.4
  14.4 0.1 copy.10
  14.5 0.0 copy-start
  14.6 0.9 true_power.1
  15.5 0.1 collective-permute-start
  15.6 0.0 copy-done.3
  15.6 0.1 fusion.3
  15.7 0.1 fusion.2
  15.8 0.0 copy-done.4
  15.8 0.1 fusion.1
  15.9 0.1 pad_add_fusion.1
  15.9 0.1 reshape.9
  16.1 0.1 fusion
  16.2 0.1 pad_maximum_fusion.1
  16.2 0.1 reshape.10
  16.3 0.4 collective-permute-done
  16.8 3.0 %collective-permute-start.3 = (f32[8,128]{1,0:T(8,128)S(1)}, f32[8,128]{1,0:T(8,128)S(1)}, u32[]{:S(2)}, u32[]{:S(2)}) collective-permute-start(f32[8,128]{1,0:T(8,128)S(1)} %add.18.refs_0_), channel_id=1, source_target_pairs={{0,6},{1,7},{2,0},{3,1},{4,2},{5,3},{6,4},{7,5},{8,14},{9,15},{10,... | collective-permute-start | bytes 12296 | tf_op jit(solution)/shard_map/ppermute | solution.py:293
  19.8 0.6 collective-permute-start.2
  20.4 1.0 collective-permute-start.1
  21.4 0.0 collective-permute-done.3.refs_3_
  21.4 3.5 %collective-permute-done.2.refs_2_ = f32[8,128]{1,0:T(8,128)S(1)} collective-permute-done((f32[8,128]{1,0:T(8,128)S(1)}, f32[8,128]{1,0:T(8,128)S(1)}, u32[]{:S(2)}, u32[]{:S(2)}) %collective-permute-start.2) | collective-permute-done | bytes 4128 | tf_op jit(solution)/shard_map/ppermute | solution.py:293
  24.9 0.3 collective-permute-done.1.refs_1_
  25.2 4.3 %all-to-all-done.buf_ref = bf16[32,56,128]{2,1,0:T(8,128)(2,1)} async-done(((bf16[32,56,128]{2,1,0:T(8,128)(2,1)}), bf16[32,56,128]{2,1,0:T(8,128)(2,1)}, u32[]{:S(2)}, u32[]{:S(2)}) %all-to-all-start) | async-done | bytes 458784 | tf_op jit(solution)/shard_map/all_to_all | solution.py:286
  29.6 20.4 %gather.1 = (bf16[512,768]{1,0:T(8,128)(2,1)S(1)}, f32[8,128]{1,0:T(8,128)S(1)}) custom-call(bf16[32,56,128]{2,1,0:T(8,128)(2,1)} %all-to-all-done.buf_ref, s32[3,9,1280]{2,1,0:T(8,128)S(1)} %pad_add_fusion.cell_ref, f32[3,9,1280]{2,1,0:T(8,128)S(1)} %pad_maximum_fusion.weight_ref, f32[8,128]{1,0:T(8,128)S(1)} %add.18.refs_0_, ...), custom_call_target="tpu_custom_call" | custom-call | tf_op jit(solution)/shard_map/gather/pallas_call | solution.py:345
  50.0 0.0 copy-done
  50.0 2.0 %spectrum.1 = (bf16[256,1280]{1,0:T(8,128)(2,1)S(1)}, f32[32,1,2048]{2,1,0:T(1,128)S(1)}) custom-call(f32[8]{0:T(128)S(1)} %add_cosine_fusion.lat_ref, bf16[512,768]{1,0:T(8,128)(2,1)S(1)} %get-tuple-element.22.grid_ref, bf16[1280,768]{1,0:T(8,128)(2,1)S(1)} %copy-done, bf16[256,1280]{1,0:T(8,128)(2,1)S(1)} %bitcast.7, ...), custom_call_target="tpu_custom_call" | custom-call | tf_op jit(solution)/shard_map/spectrum/pallas_call | solution.py:362
  52.0 16.6 %all_to_all.20.parts_ref = f32[32,1,2048]{2,1,0:T(1,128)S(1)} all-to-all(f32[32,1,2048]{2,1,0:T(1,128)S(1)} %get-tuple-element.26), channel_id=1, replica_groups=mesh['band'=32,'chan'=8] {'band'}, dimensions={0} | all-to-all | bytes 524288 | tf_op jit(solution)/shard_map/all_to_all | solution.py:286
  68.6 0.2 middle.1
  68.8 14.4 %all_to_all.21.factor_ref = f32[32,1,1280]{2,1,0:T(1,128)S(1)} all-to-all(f32[32,1,1280]{2,1,0:T(1,128)S(1)} %middle.1), channel_id=1, replica_groups=mesh['band'=32,'chan'=8] {'band'}, dimensions={0} | all-to-all | bytes 327680 | tf_op jit(solution)/shard_map/all_to_all | solution.py:286
  83.3 0.0 copy-start.1
  83.3 20.0 %backward.1 = bf16[32,56,128]{2,1,0:T(8,128)(2,1)S(1)} custom-call(f32[8]{0:T(128)S(1)} %add_cosine_fusion.lat_ref, s32[3,9,1280]{2,1,0:T(8,128)S(1)} %pad_add_fusion.cell_ref, f32[3,9,1280]{2,1,0:T(8,128)S(1)} %pad_maximum_fusion.weight_ref, bf16[1280,768]{1,0:T(8,128)(2,1)S(1)} %copy-done, bf16[256,1280]{1,0:T(8,128)(2,1)S(1)} %bitcast.8, ...), custom_call_target="tpu_custom_call" | custom-call | tf_op jit(solution)/shard_map/backward/pallas_call | solution.py:385
  103.3 17.9 %all_to_all.22.blocks_ref = bf16[32,56,128]{2,1,0:T(8,128)(2,1)S(1)} all-to-all(bf16[32,56,128]{2,1,0:T(8,128)(2,1)S(1)} %backward.1), channel_id=1, replica_groups=mesh['band'=32,'chan'=8] {'band'}, dimensions={0} | all-to-all | bytes 917504 | tf_op jit(solution)/shard_map/all_to_all | solution.py:286
  121.2 0.0 copy-done.1
  121.2 1.4 %unpack.1 = bf16[28,4096]{1,0:T(8,128)(2,1)} custom-call(s32[32]{0:T(128)S(1)} %copy-done.1, bf16[32,56,128]{2,1,0:T(8,128)(2,1)S(1)} %all_to_all.22.blocks_ref), custom_call_target="tpu_custom_call" | custom-call | tf_op jit(solution)/shard_map/unpack/pallas_call | solution.py:400
  (5 shorter events, 0.1 us)
Async XLA Ops:
  0.0 14.0 %copy-start.2 = (bf16[1,28,8,2,640]{4,3,2,1,0:T(2,128)(2,1)S(1)}, bf16[1,28,8,2,640]{4,3,2,1,0:T(2,128)(2,1)}, u32[]{:S(2)}) copy-start(bf16[1,28,8,2,640]{4,3,2,1,0:T(2,128)(2,1)} %param.11) | copy-start | bytes 1720324
  2.0 27.5 %all-to-all-start = ((bf16[32,56,128]{2,1,0:T(8,128)(2,1)}), bf16[32,56,128]{2,1,0:T(8,128)(2,1)}, u32[]{:S(2)}, u32[]{:S(2)}) async-start(bf16[32,56,128]{2,1,0:T(8,128)(2,1)} %pack.1), calls=%async_computation | async-start | bytes 917504 | tf_op jit(solution)/shard_map/all_to_all | solution.py:286
  14.0 1.6 %copy-start.3 = (s32[3,8,1440]{2,1,0:T(8,128)S(1)}, s32[3,8,1440]{2,1,0:T(8,128)}, u32[]{:S(2)}) copy-start(s32[3,8,1440]{2,1,0:T(8,128)} %param.9) | copy-start | bytes 414724
  14.4 1.4 %copy-start.4 = (f32[3,8,1440]{2,1,0:T(8,128)S(1)}, f32[3,8,1440]{2,1,0:T(8,128)}, u32[]{:S(2)}) copy-start(f32[3,8,1440]{2,1,0:T(8,128)} %param.10) | copy-start | bytes 414724
  14.5 35.5 %copy-start = (bf16[1280,768]{1,0:T(8,128)(2,1)S(1)}, bf16[1280,768]{1,0:T(8,128)(2,1)}, u32[]{:S(2)}) copy-start(bf16[1280,768]{1,0:T(8,128)(2,1)} %constant.20.clone.table_ref) | copy-start | bytes 5898244
  15.5 1.3 %collective-permute-start = (f32[8,128]{1,0:T(8,128)S(1)}, f32[8,128]{1,0:T(8,128)S(1)}, u32[]{:S(2)}, u32[]{:S(2)}) collective-permute-start(f32[8,128]{1,0:T(8,128)S(1)} %get-tuple-element.21), channel_id=1, source_target_pairs={{0,1},{1,0},{2,3},{3,2},{4,5},{5,4},{6,7},{7,6},{8,9},{9,8},{10,11... | collective-permute-start | bytes 12296 | tf_op jit(solution)/shard_map/ppermute | solution.py:291
  16.8 4.6 %collective-permute-start.3 = (f32[8,128]{1,0:T(8,128)S(1)}, f32[8,128]{1,0:T(8,128)S(1)}, u32[]{:S(2)}, u32[]{:S(2)}) collective-permute-start(f32[8,128]{1,0:T(8,128)S(1)} %add.18.refs_0_), channel_id=1, source_target_pairs={{0,6},{1,7},{2,0},{3,1},{4,2},{5,3},{6,4},{7,5},{8,14},{9,15},{10,... | collective-permute-start | bytes 12296 | tf_op jit(solution)/shard_map/ppermute | solution.py:293
  19.8 5.1 %collective-permute-start.2 = (f32[8,128]{1,0:T(8,128)S(1)}, f32[8,128]{1,0:T(8,128)S(1)}, u32[]{:S(2)}, u32[]{:S(2)}) collective-permute-start(f32[8,128]{1,0:T(8,128)S(1)} %add.18.refs_0_), channel_id=1, source_target_pairs={{0,4},{1,5},{2,6},{3,7},{4,0},{5,1},{6,2},{7,3},{8,12},{9,13},{10,... | collective-permute-start | bytes 12296 | tf_op jit(solution)/shard_map/ppermute | solution.py:293
  20.4 4.8 %collective-permute-start.1 = (f32[8,128]{1,0:T(8,128)S(1)}, f32[8,128]{1,0:T(8,128)S(1)}, u32[]{:S(2)}, u32[]{:S(2)}) collective-permute-start(f32[8,128]{1,0:T(8,128)S(1)} %add.18.refs_0_), channel_id=1, source_target_pairs={{0,2},{1,3},{2,4},{3,5},{4,6},{5,7},{6,0},{7,1},{8,10},{9,11},{10,... | collective-permute-start | bytes 12296 | tf_op jit(solution)/shard_map/ppermute | solution.py:293
  83.3 37.9 %copy-start.1 = (s32[32]{0:T(128)S(1)}, s32[32]{0:T(128)}, u32[]{:S(2)}) copy-start(s32[32]{0:T(128)} %slot_ref.3) | copy-start | bytes 388

commit v6 on v5

--- a/solution.py
+++ b/solution.py
@@ -176,7 +176,7 @@
             grid[pl.ds(pl.multiple_of(a * CP, CP), CP), cols] = total.astype(jnp.bfloat16)
         return 0
 
-    lax.fori_loop(0, CELL_ROWS, row, 0)
+    lax.fori_loop(0, CELL_ROWS, row, 0, unroll=3)
     rest = grid[ROWS : ROWS + CP, :].astype(jnp.float32)
     zeros = jnp.zeros((CP, HALF_PAD - HALF_LON), jnp.float32)
     for a in range(LAT_DEV):
@@ -260,7 +260,7 @@
                 )
         return 0
 
-    lax.fori_loop(0, CELL_ROWS, row, 0)
+    lax.fori_loop(0, CELL_ROWS, row, 0, unroll=3)
     first = first_rows(NB)
     for p in range(owners // 2):
         block = total[p * PAIR : (p + 1) * PAIR, :]

time: 123 us -> 121 us (0.984)
  Pallas kernels: 47 us -> 44.8 us
    pallas_call x1, Pallas kernels: 20 us -> 18.7 us  [shards(): pl.pallas_call(functools.partial(backward_kernel, owners), out_shape=jax....]
where the time goes in v6:
time: 121 us; the launch traced here: 120 us
  blocking collectives  49 us (40%)
  Pallas kernels  44.8 us (37%)
  starting transfers between devices  15.9 us (13%)
  waiting for transfers between devices  8.56 us (7%)
  local copies, waits for them, and re-layouts  1.72 us (1%)
    all_to_all x3, blocking collectives, exchange(): return lax.all_to_all(blocks, axis, split_axis=0, concat_axis=0, tiled=True)  49 us
    pallas_call x1, Pallas kernels, shards(): pl.pallas_call(functools.partial(gather_kernel, owners), out_shape=(jax.S...  19.6 us
    pallas_call x1, Pallas kernels, shards(): pl.pallas_call(functools.partial(backward_kernel, owners), out_shape=jax....  18.7 us
    all_to_all x1, starting transfers between devices, exchange(): return lax.all_to_all(blocks, axis, split_axis=0, concat_axis=0, tiled=True)  11.2 us
    ppermute x3, starting transfers between devices, everyone(): return [block] + [lax.ppermute(block, axis, shift) for shift in shifts]  4.61 us
    all_to_all x1, waiting for transfers between devices, exchange(): return lax.all_to_all(blocks, axis, split_axis=0, concat_axis=0, tiled=True)  4.3 us
    ppermute x3, waiting for transfers between devices, everyone(): return [block] + [lax.ppermute(block, axis, shift) for shift in shifts]  3.81 us
  transfers between devices with their start and end apart: 5, of which 4 were waited for; matrix products, arithmetic and copies ran while one was open for 2% of the time, Pallas kernels for 1%

profile of v6, /device:TPU:32, one launch (start us, length us, event | category | flops | bytes accessed | tf_op | source)
XLA Modules:
  0.0 120.4 jit_solution(1058272246977174970)
XLA Ops:
  0.0 0.0 copy-start.2
  0.0 2.0 %pack.1 = bf16[32,56,128]{2,1,0:T(8,128)(2,1)} custom-call(s32[32]{0:T(128)} %slot_ref.3, bf16[28,4096]{1,0:T(8,128)(2,1)} %bitcast.10), custom_call_target="tpu_custom_call" | custom-call | tf_op jit(solution)/shard_map/pack/pallas_call | solution.py:311
  2.0 11.2 %all-to-all-start = ((bf16[32,56,128]{2,1,0:T(8,128)(2,1)}), bf16[32,56,128]{2,1,0:T(8,128)(2,1)}, u32[]{:S(2)}, u32[]{:S(2)}) async-start(bf16[32,56,128]{2,1,0:T(8,128)(2,1)} %pack.1), calls=%async_computation | async-start | bytes 917504 | tf_op jit(solution)/shard_map/all_to_all | solution.py:286
  13.3 0.7 broadcast_in_dim.7.spec_weight_ref
  14.0 0.0 copy-done.2
  14.0 0.0 copy-start.3
  14.0 0.4 reshape_squeeze.3
  14.4 0.0 copy-start.4
  14.4 0.1 copy.10
  14.5 0.0 copy-start
  14.6 0.9 true_power.1
  15.5 0.1 collective-permute-start
  15.6 0.0 copy-done.3
  15.6 0.1 fusion.3
  15.7 0.1 fusion.2
  15.8 0.0 copy-done.4
  15.8 0.1 fusion.1
  15.9 0.1 pad_add_fusion.1
  15.9 0.1 reshape.9
  16.1 0.1 fusion
  16.2 0.1 pad_maximum_fusion.1
  16.2 0.1 reshape.10
  16.3 0.4 collective-permute-done
  16.8 3.0 %collective-permute-start.3 = (f32[8,128]{1,0:T(8,128)S(1)}, f32[8,128]{1,0:T(8,128)S(1)}, u32[]{:S(2)}, u32[]{:S(2)}) collective-permute-start(f32[8,128]{1,0:T(8,128)S(1)} %add.18.refs_0_), channel_id=1, source_target_pairs={{0,6},{1,7},{2,0},{3,1},{4,2},{5,3},{6,4},{7,5},{8,14},{9,15},{10,... | collective-permute-start | bytes 12296 | tf_op jit(solution)/shard_map/ppermute | solution.py:293
  19.8 0.6 collective-permute-start.2
  20.4 1.0 collective-permute-start.1
  21.4 0.0 collective-permute-done.3.refs_3_
  21.4 3.5 %collective-permute-done.2.refs_2_ = f32[8,128]{1,0:T(8,128)S(1)} collective-permute-done((f32[8,128]{1,0:T(8,128)S(1)}, f32[8,128]{1,0:T(8,128)S(1)}, u32[]{:S(2)}, u32[]{:S(2)}) %collective-permute-start.2) | collective-permute-done | bytes 4128 | tf_op jit(solution)/shard_map/ppermute | solution.py:293
  24.9 0.3 collective-permute-done.1.refs_1_
  25.2 4.3 %all-to-all-done.buf_ref = bf16[32,56,128]{2,1,0:T(8,128)(2,1)} async-done(((bf16[32,56,128]{2,1,0:T(8,128)(2,1)}), bf16[32,56,128]{2,1,0:T(8,128)(2,1)}, u32[]{:S(2)}, u32[]{:S(2)}) %all-to-all-start) | async-done | bytes 458784 | tf_op jit(solution)/shard_map/all_to_all | solution.py:286
  29.6 19.6 %gather.1 = (bf16[512,768]{1,0:T(8,128)(2,1)S(1)}, f32[8,128]{1,0:T(8,128)S(1)}) custom-call(bf16[32,56,128]{2,1,0:T(8,128)(2,1)} %all-to-all-done.buf_ref, s32[3,9,1280]{2,1,0:T(8,128)S(1)} %pad_add_fusion.cell_ref, f32[3,9,1280]{2,1,0:T(8,128)S(1)} %pad_maximum_fusion.weight_ref, f32[8,128]{1,0:T(8,128)S(1)} %add.18.refs_0_, ...), custom_call_target="tpu_custom_call" | custom-call | tf_op jit(solution)/shard_map/gather/pallas_call | solution.py:345
  49.1 0.0 copy-done
  49.1 2.0 %spectrum.1 = (bf16[256,1280]{1,0:T(8,128)(2,1)S(1)}, f32[32,1,2048]{2,1,0:T(1,128)S(1)}) custom-call(f32[8]{0:T(128)S(1)} %add_cosine_fusion.lat_ref, bf16[512,768]{1,0:T(8,128)(2,1)S(1)} %get-tuple-element.22.grid_ref, bf16[1280,768]{1,0:T(8,128)(2,1)S(1)} %copy-done, bf16[256,1280]{1,0:T(8,128)(2,1)S(1)} %bitcast.7, ...), custom_call_target="tpu_custom_call" | custom-call | tf_op jit(solution)/shard_map/spectrum/pallas_call | solution.py:362
  51.2 16.6 %all_to_all.20.parts_ref = f32[32,1,2048]{2,1,0:T(1,128)S(1)} all-to-all(f32[32,1,2048]{2,1,0:T(1,128)S(1)} %get-tuple-element.26), channel_id=1, replica_groups=mesh['band'=32,'chan'=8] {'band'}, dimensions={0} | all-to-all | bytes 524288 | tf_op jit(solution)/shard_map/all_to_all | solution.py:286
  67.7 0.2 middle.1
  68.0 14.4 %all_to_all.21.factor_ref = f32[32,1,1280]{2,1,0:T(1,128)S(1)} all-to-all(f32[32,1,1280]{2,1,0:T(1,128)S(1)} %middle.1), channel_id=1, replica_groups=mesh['band'=32,'chan'=8] {'band'}, dimensions={0} | all-to-all | bytes 327680 | tf_op jit(solution)/shard_map/all_to_all | solution.py:286
  82.4 0.0 copy-start.1
  82.4 18.7 %backward.1 = bf16[32,56,128]{2,1,0:T(8,128)(2,1)S(1)} custom-call(f32[8]{0:T(128)S(1)} %add_cosine_fusion.lat_ref, s32[3,9,1280]{2,1,0:T(8,128)S(1)} %pad_add_fusion.cell_ref, f32[3,9,1280]{2,1,0:T(8,128)S(1)} %pad_maximum_fusion.weight_ref, bf16[1280,768]{1,0:T(8,128)(2,1)S(1)} %copy-done, bf16[256,1280]{1,0:T(8,128)(2,1)S(1)} %bitcast.8, ...), custom_call_target="tpu_custom_call" | custom-call | tf_op jit(solution)/shard_map/backward/pallas_call | solution.py:385
  101.1 17.9 %all_to_all.22.blocks_ref = bf16[32,56,128]{2,1,0:T(8,128)(2,1)S(1)} all-to-all(bf16[32,56,128]{2,1,0:T(8,128)(2,1)S(1)} %backward.1), channel_id=1, replica_groups=mesh['band'=32,'chan'=8] {'band'}, dimensions={0} | all-to-all | bytes 917504 | tf_op jit(solution)/shard_map/all_to_all | solution.py:286
  119.0 0.0 copy-done.1
  119.0 1.4 %unpack.1 = bf16[28,4096]{1,0:T(8,128)(2,1)} custom-call(s32[32]{0:T(128)S(1)} %copy-done.1, bf16[32,56,128]{2,1,0:T(8,128)(2,1)S(1)} %all_to_all.22.blocks_ref), custom_call_target="tpu_custom_call" | custom-call | tf_op jit(solution)/shard_map/unpack/pallas_call | solution.py:400
  (5 shorter events, 0.1 us)
Async XLA Ops:
  0.0 14.0 %copy-start.2 = (bf16[1,28,8,2,640]{4,3,2,1,0:T(2,128)(2,1)S(1)}, bf16[1,28,8,2,640]{4,3,2,1,0:T(2,128)(2,1)}, u32[]{:S(2)}) copy-start(bf16[1,28,8,2,640]{4,3,2,1,0:T(2,128)(2,1)} %param.11) | copy-start | bytes 1720324
  2.0 27.5 %all-to-all-start = ((bf16[32,56,128]{2,1,0:T(8,128)(2,1)}), bf16[32,56,128]{2,1,0:T(8,128)(2,1)}, u32[]{:S(2)}, u32[]{:S(2)}) async-start(bf16[32,56,128]{2,1,0:T(8,128)(2,1)} %pack.1), calls=%async_computation | async-start | bytes 917504 | tf_op jit(solution)/shard_map/all_to_all | solution.py:286
  14.0 1.6 %copy-start.3 = (s32[3,8,1440]{2,1,0:T(8,128)S(1)}, s32[3,8,1440]{2,1,0:T(8,128)}, u32[]{:S(2)}) copy-start(s32[3,8,1440]{2,1,0:T(8,128)} %param.9) | copy-start | bytes 414724
  14.4 1.4 %copy-start.4 = (f32[3,8,1440]{2,1,0:T(8,128)S(1)}, f32[3,8,1440]{2,1,0:T(8,128)}, u32[]{:S(2)}) copy-start(f32[3,8,1440]{2,1,0:T(8,128)} %param.10) | copy-start | bytes 414724
  14.5 34.6 %copy-start = (bf16[1280,768]{1,0:T(8,128)(2,1)S(1)}, bf16[1280,768]{1,0:T(8,128)(2,1)}, u32[]{:S(2)}) copy-start(bf16[1280,768]{1,0:T(8,128)(2,1)} %constant.20.clone.table_ref) | copy-start | bytes 5898244
  15.5 1.3 %collective-permute-start = (f32[8,128]{1,0:T(8,128)S(1)}, f32[8,128]{1,0:T(8,128)S(1)}, u32[]{:S(2)}, u32[]{:S(2)}) collective-permute-start(f32[8,128]{1,0:T(8,128)S(1)} %get-tuple-element.21), channel_id=1, source_target_pairs={{0,1},{1,0},{2,3},{3,2},{4,5},{5,4},{6,7},{7,6},{8,9},{9,8},{10,11... | collective-permute-start | bytes 12296 | tf_op jit(solution)/shard_map/ppermute | solution.py:291
  16.8 4.6 %collective-permute-start.3 = (f32[8,128]{1,0:T(8,128)S(1)}, f32[8,128]{1,0:T(8,128)S(1)}, u32[]{:S(2)}, u32[]{:S(2)}) collective-permute-start(f32[8,128]{1,0:T(8,128)S(1)} %add.18.refs_0_), channel_id=1, source_target_pairs={{0,6},{1,7},{2,0},{3,1},{4,2},{5,3},{6,4},{7,5},{8,14},{9,15},{10,... | collective-permute-start | bytes 12296 | tf_op jit(solution)/shard_map/ppermute | solution.py:293
  19.8 5.1 %collective-permute-start.2 = (f32[8,128]{1,0:T(8,128)S(1)}, f32[8,128]{1,0:T(8,128)S(1)}, u32[]{:S(2)}, u32[]{:S(2)}) collective-permute-start(f32[8,128]{1,0:T(8,128)S(1)} %add.18.refs_0_), channel_id=1, source_target_pairs={{0,4},{1,5},{2,6},{3,7},{4,0},{5,1},{6,2},{7,3},{8,12},{9,13},{10,... | collective-permute-start | bytes 12296 | tf_op jit(solution)/shard_map/ppermute | solution.py:293
  20.4 4.8 %collective-permute-start.1 = (f32[8,128]{1,0:T(8,128)S(1)}, f32[8,128]{1,0:T(8,128)S(1)}, u32[]{:S(2)}, u32[]{:S(2)}) collective-permute-start(f32[8,128]{1,0:T(8,128)S(1)} %add.18.refs_0_), channel_id=1, source_target_pairs={{0,2},{1,3},{2,4},{3,5},{4,6},{5,7},{6,0},{7,1},{8,10},{9,11},{10,... | collective-permute-start | bytes 12296 | tf_op jit(solution)/shard_map/ppermute | solution.py:293
  82.4 36.6 %copy-start.1 = (s32[32]{0:T(128)S(1)}, s32[32]{0:T(128)}, u32[]{:S(2)}) copy-start(s32[32]{0:T(128)} %slot_ref.3) | copy-start | bytes 388

commit v7 on v6

--- a/solution.py
+++ b/solution.py
@@ -134,10 +134,10 @@
     return jnp.where((owner & 1) == wanted, owner >> 1, -1)
 
 
-def gather_kernel(owners, buf_ref, cell_ref, weight_ref, *refs):
-    energy_refs = refs[:-5]
-    grid_ref, energy_ref, staged, nodes, grid = refs[-5:]
-    energy_ref[...] = sum((ref[...] for ref in energy_refs[1:]), energy_refs[0][...])
+def forward_kernel(owners, lat_ref, buf_ref, cell_ref, weight_ref, table_ref, target_ref,
+                   true_ref, *refs):
+    energy_refs = refs[:-6]
+    spec_ref, sums_ref, staged, nodes, grid, half_rows = refs[-6:]
     first = first_rows(NB)
     for p in range(owners // 2):
         even = buf_ref[2 * p].astype(jnp.float32)
@@ -184,16 +184,12 @@
             at = a * REST + h * HALF_REST
             piece = jnp.concatenate([rest[:, at : at + HALF_REST], zeros], axis=1)
             rows = slice(h * ROWS + a * CP, h * ROWS + (a + 1) * CP)
-            grid_ref[rows, HALF_MAIN:] = piece.astype(jnp.bfloat16)
+            half_rows[rows, HALF_MAIN:] = piece.astype(jnp.bfloat16)
     for h in range(2):
         columns = slice(h * HALF_MAIN, (h + 1) * HALF_MAIN)
-        grid_ref[h * ROWS : (h + 1) * ROWS, :HALF_MAIN] = grid[:ROWS, columns]
-
-
-def spectrum_kernel(lat_ref, grid_ref, table_ref, target_ref, true_ref, energy_ref, spec_ref,
-                    sums_ref):
+        half_rows[h * ROWS : (h + 1) * ROWS, :HALF_MAIN] = grid[:ROWS, columns]
     halves = lax.dot_general(
-        grid_ref[...], table_ref[...], (((1,), (1,)), ((), ())),
+        half_rows[...], table_ref[...], (((1,), (1,)), ((), ())),
         preferred_element_type=jnp.float32,
     )
     spectrum = halves[:ROWS] + half_sign() * halves[ROWS:]
@@ -209,7 +205,8 @@
     sums_ref[:, 0, :K] = pred[:, :K] + pred[:, K:]
     sums_ref[:, 0, K : 2 * K] = true_ref[...]
     sums_ref[:, 0, 2 * K : 3 * K] = cross[:, :K] + cross[:, K:]
-    sums_ref[:, 0, 3 * K :] = jnp.broadcast_to(energy_ref[0:1, :], (CP, NB))
+    energy = sum((ref[0:1, :] for ref in energy_refs[1:]), energy_refs[0][0:1, :])
+    sums_ref[:, 0, 3 * K :] = jnp.broadcast_to(energy, (CP, NB))
 
 
 def backward_kernel(owners, lat_ref, cell_ref, weight_ref, table_ref, target_ref, spec_ref,
@@ -342,34 +339,23 @@
     )(lat_weight, spec_weight[None, :], target)
     energies = everyone(energy_part, "chan")
 
-    grid, energy = pl.pallas_call(
-        functools.partial(gather_kernel, owners),
+    spectrum, sums = pl.pallas_call(
+        functools.partial(forward_kernel, owners),
         out_shape=(
-            jax.ShapeDtypeStruct((2 * ROWS, HALF_PAD), jnp.bfloat16),
-            jax.ShapeDtypeStruct(energy_part.shape, jnp.float32),
+            jax.ShapeDtypeStruct((ROWS, 2 * K), jnp.bfloat16),
+            jax.ShapeDtypeStruct((CP, 1, 3 * K + NB), jnp.float32),
         ),
-        in_specs=[VMEM] * (3 + len(energies)),
+        in_specs=[SMEM] + [VMEM] * (6 + len(energies)),
         out_specs=(VMEM, VMEM),
         scratch_shapes=[
             pltpu.VMEM((owners * CHANS, LO), jnp.float32),
             pltpu.VMEM((owners * CHANS, LO), jnp.bfloat16),
             pltpu.VMEM((CELL_ROWS * CP, MAIN), jnp.bfloat16),
+            pltpu.VMEM((2 * ROWS, HALF_PAD), jnp.bfloat16),
         ],
         compiler_params=PARAMS,
-        name="gather",
-    )(received, refs, weights, *energies)
-
-    spectrum, sums = pl.pallas_call(
-        spectrum_kernel,
-        out_shape=(
-            jax.ShapeDtypeStruct((ROWS, 2 * K), jnp.bfloat16),
-            jax.ShapeDtypeStruct((CP, 1, 3 * K + NB), jnp.float32),
-        ),
-        in_specs=[SMEM] + [VMEM] * 5,
-        out_specs=(VMEM, VMEM),
-        compiler_params=PARAMS,
-        name="spectrum",
-    )(lat_weight, grid, table, target, true_part, energy)
+        name="forward",
+    )(lat_weight, received, refs, weights, table, target, true_part, *energies)
 
     parts = exchange(sums, "band")
     factors = pl.pallas_call(

time: 121 us -> 120 us (level)
    pallas_call x2 -> x1, Pallas kernels: 21.6 us -> 20.9 us  [shards(): pl.pallas_call(functools.partial(forward_kernel, owners), out_shape=(jax....]
where the time goes in v7:
time: 120 us
  blocking collectives  48.9 us (41%)
  Pallas kernels  44.2 us (37%)
  starting transfers between devices  15.9 us (13%)
  waiting for transfers between devices  8.56 us (7%)
  local copies, waits for them, and re-layouts  1.72 us (1%)
    all_to_all x3, blocking collectives, exchange(): return lax.all_to_all(blocks, axis, split_axis=0, concat_axis=0, tiled=True)  48.9 us
    pallas_call x1, Pallas kernels, shards(): pl.pallas_call(functools.partial(forward_kernel, owners), out_shape=(jax....  20.9 us
    pallas_call x1, Pallas kernels, shards(): pl.pallas_call(functools.partial(backward_kernel, owners), out_shape=jax....  18.7 us
    all_to_all x1, starting transfers between devices, exchange(): return lax.all_to_all(blocks, axis, split_axis=0, concat_axis=0, tiled=True)  11.2 us
    ppermute x3, starting transfers between devices, everyone(): return [block] + [lax.ppermute(block, axis, shift) for shift in shifts]  4.61 us
    all_to_all x1, waiting for transfers between devices, exchange(): return lax.all_to_all(blocks, axis, split_axis=0, concat_axis=0, tiled=True)  4.31 us
    ppermute x3, waiting for transfers between devices, everyone(): return [block] + [lax.ppermute(block, axis, shift) for shift in shifts]  3.81 us
  transfers between devices with their start and end apart: 5, of which 4 were waited for; matrix products, arithmetic and copies ran while one was open for 2% of the time, Pallas kernels for 1%

profile of v7, /device:TPU:32, one launch (start us, length us, event | category | flops | bytes accessed | tf_op | source)
XLA Modules:
  0.0 119.7 jit_solution(7643635879594673615)
XLA Ops:
  0.0 0.0 copy-start.2
  0.0 2.1 %pack.1 = bf16[32,56,128]{2,1,0:T(8,128)(2,1)} custom-call(s32[32]{0:T(128)} %slot_ref.3, bf16[28,4096]{1,0:T(8,128)(2,1)} %bitcast.10), custom_call_target="tpu_custom_call" | custom-call | tf_op jit(solution)/shard_map/pack/pallas_call | solution.py:308
  2.1 11.2 %all-to-all-start = ((bf16[32,56,128]{2,1,0:T(8,128)(2,1)}), bf16[32,56,128]{2,1,0:T(8,128)(2,1)}, u32[]{:S(2)}, u32[]{:S(2)}) async-start(bf16[32,56,128]{2,1,0:T(8,128)(2,1)} %pack.1), calls=%async_computation | async-start | bytes 917504 | tf_op jit(solution)/shard_map/all_to_all | solution.py:283
  13.4 0.7 broadcast_in_dim.7.spec_weight_ref
  14.0 0.0 copy-done.2
  14.1 0.0 copy-start.3
  14.1 0.4 reshape_squeeze.3
  14.4 0.0 copy-start.4
  14.4 0.1 copy.10
  14.5 0.0 copy-start
  14.6 0.9 true_power.1
  15.5 0.1 collective-permute-start
  15.6 0.0 copy-done.3
  15.6 0.1 fusion.3
  15.7 0.1 fusion.2
  15.8 0.0 copy-done.4
  15.8 0.1 fusion.1
  15.9 0.1 pad_add_fusion.1
  16.0 0.1 reshape.9
  16.1 0.1 fusion
  16.2 0.1 pad_maximum_fusion.1
  16.2 0.1 reshape.10
  16.3 0.4 collective-permute-done
  16.8 3.0 %collective-permute-start.3 = (f32[8,128]{1,0:T(8,128)S(1)}, f32[8,128]{1,0:T(8,128)S(1)}, u32[]{:S(2)}, u32[]{:S(2)}) collective-permute-start(f32[8,128]{1,0:T(8,128)S(1)} %add.18.refs_0_), channel_id=1, source_target_pairs={{0,6},{1,7},{2,0},{3,1},{4,2},{5,3},{6,4},{7,5},{8,14},{9,15},{10,... | collective-permute-start | bytes 12296 | tf_op jit(solution)/shard_map/ppermute | solution.py:290
  19.8 0.6 collective-permute-start.2
  20.4 1.0 collective-permute-start.1
  21.4 0.0 collective-permute-done.3.refs_3_
  21.4 3.5 %collective-permute-done.2.refs_2_ = f32[8,128]{1,0:T(8,128)S(1)} collective-permute-done((f32[8,128]{1,0:T(8,128)S(1)}, f32[8,128]{1,0:T(8,128)S(1)}, u32[]{:S(2)}, u32[]{:S(2)}) %collective-permute-start.2) | collective-permute-done | bytes 4128 | tf_op jit(solution)/shard_map/ppermute | solution.py:290
  24.9 0.3 collective-permute-done.1.refs_1_
  25.3 4.3 %all-to-all-done.buf_ref = bf16[32,56,128]{2,1,0:T(8,128)(2,1)} async-done(((bf16[32,56,128]{2,1,0:T(8,128)(2,1)}), bf16[32,56,128]{2,1,0:T(8,128)(2,1)}, u32[]{:S(2)}, u32[]{:S(2)}) %all-to-all-start) | async-done | bytes 458784 | tf_op jit(solution)/shard_map/all_to_all | solution.py:283
  29.6 0.0 copy-done
  29.6 20.9 %forward.1 = (bf16[256,1280]{1,0:T(8,128)(2,1)S(1)}, f32[32,1,2048]{2,1,0:T(1,128)S(1)}) custom-call(f32[8]{0:T(128)S(1)} %add_cosine_fusion.lat_ref, bf16[32,56,128]{2,1,0:T(8,128)(2,1)} %all-to-all-done.buf_ref, s32[3,9,1280]{2,1,0:T(8,128)S(1)} %pad_add_fusion.cell_ref, f32[3,9,1280]{2,1,0:T(8,128)S(1)} %pad_maximum_fusion.weight_ref, ...), custom_call_target="tpu_custom_call" | custom-call | tf_op jit(solution)/shard_map/forward/pallas_call | solution.py:342
  50.5 16.6 %all_to_all.20.parts_ref = f32[32,1,2048]{2,1,0:T(1,128)S(1)} all-to-all(f32[32,1,2048]{2,1,0:T(1,128)S(1)} %get-tuple-element.22), channel_id=1, replica_groups=mesh['band'=32,'chan'=8] {'band'}, dimensions={0} | all-to-all | bytes 524288 | tf_op jit(solution)/shard_map/all_to_all | solution.py:283
  67.1 0.2 middle.1
  67.3 14.4 %all_to_all.21.factor_ref = f32[32,1,1280]{2,1,0:T(1,128)S(1)} all-to-all(f32[32,1,1280]{2,1,0:T(1,128)S(1)} %middle.1), channel_id=1, replica_groups=mesh['band'=32,'chan'=8] {'band'}, dimensions={0} | all-to-all | bytes 327680 | tf_op jit(solution)/shard_map/all_to_all | solution.py:283
  81.7 0.0 copy-start.1
  81.7 18.7 %backward.1 = bf16[32,56,128]{2,1,0:T(8,128)(2,1)S(1)} custom-call(f32[8]{0:T(128)S(1)} %add_cosine_fusion.lat_ref, s32[3,9,1280]{2,1,0:T(8,128)S(1)} %pad_add_fusion.cell_ref, f32[3,9,1280]{2,1,0:T(8,128)S(1)} %pad_maximum_fusion.weight_ref, bf16[1280,768]{1,0:T(8,128)(2,1)S(1)} %copy-done, bf16[256,1280]{1,0:T(8,128)(2,1)S(1)} %bitcast.8, ...), custom_call_target="tpu_custom_call" | custom-call | tf_op jit(solution)/shard_map/backward/pallas_call | solution.py:371
  100.4 17.9 %all_to_all.22.blocks_ref = bf16[32,56,128]{2,1,0:T(8,128)(2,1)S(1)} all-to-all(bf16[32,56,128]{2,1,0:T(8,128)(2,1)S(1)} %backward.1), channel_id=1, replica_groups=mesh['band'=32,'chan'=8] {'band'}, dimensions={0} | all-to-all | bytes 917504 | tf_op jit(solution)/shard_map/all_to_all | solution.py:283
  118.3 0.0 copy-done.1
  118.3 1.4 %unpack.1 = bf16[28,4096]{1,0:T(8,128)(2,1)} custom-call(s32[32]{0:T(128)S(1)} %copy-done.1, bf16[32,56,128]{2,1,0:T(8,128)(2,1)S(1)} %all_to_all.22.blocks_ref), custom_call_target="tpu_custom_call" | custom-call | tf_op jit(solution)/shard_map/unpack/pallas_call | solution.py:386
  (5 shorter events, 0.1 us)
Async XLA Ops:
  0.0 14.0 %copy-start.2 = (bf16[1,28,8,2,640]{4,3,2,1,0:T(2,128)(2,1)S(1)}, bf16[1,28,8,2,640]{4,3,2,1,0:T(2,128)(2,1)}, u32[]{:S(2)}) copy-start(bf16[1,28,8,2,640]{4,3,2,1,0:T(2,128)(2,1)} %param.11) | copy-start | bytes 1720324
  2.1 27.5 %all-to-all-start = ((bf16[32,56,128]{2,1,0:T(8,128)(2,1)}), bf16[32,56,128]{2,1,0:T(8,128)(2,1)}, u32[]{:S(2)}, u32[]{:S(2)}) async-start(bf16[32,56,128]{2,1,0:T(8,128)(2,1)} %pack.1), calls=%async_computation | async-start | bytes 917504 | tf_op jit(solution)/shard_map/all_to_all | solution.py:283
  14.1 1.6 %copy-start.3 = (s32[3,8,1440]{2,1,0:T(8,128)S(1)}, s32[3,8,1440]{2,1,0:T(8,128)}, u32[]{:S(2)}) copy-start(s32[3,8,1440]{2,1,0:T(8,128)} %param.9) | copy-start | bytes 414724
  14.4 1.4 %copy-start.4 = (f32[3,8,1440]{2,1,0:T(8,128)S(1)}, f32[3,8,1440]{2,1,0:T(8,128)}, u32[]{:S(2)}) copy-start(f32[3,8,1440]{2,1,0:T(8,128)} %param.10) | copy-start | bytes 414724
  14.5 15.0 %copy-start = (bf16[1280,768]{1,0:T(8,128)(2,1)S(1)}, bf16[1280,768]{1,0:T(8,128)(2,1)}, u32[]{:S(2)}) copy-start(bf16[1280,768]{1,0:T(8,128)(2,1)} %constant.20.clone.table_ref) | copy-start | bytes 5898244
  15.5 1.3 %collective-permute-start = (f32[8,128]{1,0:T(8,128)S(1)}, f32[8,128]{1,0:T(8,128)S(1)}, u32[]{:S(2)}, u32[]{:S(2)}) collective-permute-start(f32[8,128]{1,0:T(8,128)S(1)} %get-tuple-element.20), channel_id=1, source_target_pairs={{0,1},{1,0},{2,3},{3,2},{4,5},{5,4},{6,7},{7,6},{8,9},{9,8},{10,11... | collective-permute-start | bytes 12296 | tf_op jit(solution)/shard_map/ppermute | solution.py:288
  16.8 4.6 %collective-permute-start.3 = (f32[8,128]{1,0:T(8,128)S(1)}, f32[8,128]{1,0:T(8,128)S(1)}, u32[]{:S(2)}, u32[]{:S(2)}) collective-permute-start(f32[8,128]{1,0:T(8,128)S(1)} %add.18.refs_0_), channel_id=1, source_target_pairs={{0,6},{1,7},{2,0},{3,1},{4,2},{5,3},{6,4},{7,5},{8,14},{9,15},{10,... | collective-permute-start | bytes 12296 | tf_op jit(solution)/shard_map/ppermute | solution.py:290
  19.8 5.1 %collective-permute-start.2 = (f32[8,128]{1,0:T(8,128)S(1)}, f32[8,128]{1,0:T(8,128)S(1)}, u32[]{:S(2)}, u32[]{:S(2)}) collective-permute-start(f32[8,128]{1,0:T(8,128)S(1)} %add.18.refs_0_), channel_id=1, source_target_pairs={{0,4},{1,5},{2,6},{3,7},{4,0},{5,1},{6,2},{7,3},{8,12},{9,13},{10,... | collective-permute-start | bytes 12296 | tf_op jit(solution)/shard_map/ppermute | solution.py:290
  20.4 4.8 %collective-permute-start.1 = (f32[8,128]{1,0:T(8,128)S(1)}, f32[8,128]{1,0:T(8,128)S(1)}, u32[]{:S(2)}, u32[]{:S(2)}) collective-permute-start(f32[8,128]{1,0:T(8,128)S(1)} %add.18.refs_0_), channel_id=1, source_target_pairs={{0,2},{1,3},{2,4},{3,5},{4,6},{5,7},{6,0},{7,1},{8,10},{9,11},{10,... | collective-permute-start | bytes 12296 | tf_op jit(solution)/shard_map/ppermute | solution.py:290
  81.7 36.6 %copy-start.1 = (s32[32]{0:T(128)S(1)}, s32[32]{0:T(128)}, u32[]{:S(2)}) copy-start(s32[32]{0:T(128)} %slot_ref.3) | copy-start | bytes 388

commit v8 on v7

--- a/solution.py
+++ b/solution.py
@@ -77,13 +77,12 @@
     out_ref[...] = staged[...].astype(jnp.bfloat16)
 
 
-def unpack_kernel(slot_ref, blocks_ref, out_ref, staged):
-    staged[...] = blocks_ref[...].astype(jnp.float32)
+def unpack_kernel(slot_ref, blocks_ref, out_ref):
     for i in range(NBLK_DEV):
         owner, slot = slot_ref[i] >> 1, slot_ref[i] & 1
-        at = pl.multiple_of(slot * (BODY + 2 * HALF), 8)
-        body = staged[owner, pl.ds(at, BODY), :]
-        shared = staged[owner, BODY : BODY + 2 * HALF, :]
+        rows = blocks_ref[owner].astype(jnp.float32)
+        shared = rows[BODY : BODY + 2 * HALF]
+        body = jnp.where(slot == 0, rows[:BODY], rows[BODY + 2 * HALF :])
         last = jnp.where(slot == 0, shared, pltpu.roll(shared, HALF, 0))[:HALF]
         block = jnp.concatenate([body, last], axis=0)
         out_ref[:, i * NB : (i + 1) * NB] = block.astype(jnp.bfloat16)
@@ -388,7 +387,6 @@
         out_shape=jax.ShapeDtypeStruct((chans, nodes_local), jnp.bfloat16),
         in_specs=[SMEM, VMEM],
         out_specs=VMEM,
-        scratch_shapes=[pltpu.VMEM((owners, PAIR, NB), jnp.float32)],
         compiler_params=PARAMS,
         name="unpack",
     )(block_slot, returned)

time: 120 us -> 120 us (level)
  no operation moved by 1% of the time
where the time goes in v8:
time: 120 us
  blocking collectives  48.9 us (41%)
  Pallas kernels  44.1 us (37%)
  starting transfers between devices  15.9 us (13%)
  waiting for transfers between devices  8.56 us (7%)
  local copies, waits for them, and re-layouts  1.72 us (1%)
    all_to_all x3, blocking collectives, exchange(): return lax.all_to_all(blocks, axis, split_axis=0, concat_axis=0, tiled=True)  48.9 us
    pallas_call x1, Pallas kernels, shards(): pl.pallas_call(functools.partial(forward_kernel, owners), out_shape=(jax....  20.9 us
    pallas_call x1, Pallas kernels, shards(): pl.pallas_call(functools.partial(backward_kernel, owners), out_shape=jax....  18.7 us
    all_to_all x1, starting transfers between devices, exchange(): return lax.all_to_all(blocks, axis, split_axis=0, concat_axis=0, tiled=True)  11.2 us
    ppermute x3, starting transfers between devices, everyone(): return [block] + [lax.ppermute(block, axis, shift) for shift in shifts]  4.61 us
    all_to_all x1, waiting for transfers between devices, exchange(): return lax.all_to_all(blocks, axis, split_axis=0, concat_axis=0, tiled=True)  4.31 us
    ppermute x3, waiting for transfers between devices, everyone(): return [block] + [lax.ppermute(block, axis, shift) for shift in shifts]  3.81 us
  transfers between devices with their start and end apart: 5, of which 4 were waited for; matrix products, arithmetic and copies ran while one was open for 2% of the time, Pallas kernels for 1%

profile of v8, /device:TPU:32, one launch (start us, length us, event | category | flops | bytes accessed | tf_op | source)
XLA Modules:
  0.0 119.7 jit_solution(14778445178478686452)
XLA Ops:
  0.0 0.0 copy-start.2
  0.0 2.1 %pack.1 = bf16[32,56,128]{2,1,0:T(8,128)(2,1)} custom-call(s32[32]{0:T(128)} %slot_ref.3, bf16[28,4096]{1,0:T(8,128)(2,1)} %bitcast.10), custom_call_target="tpu_custom_call" | custom-call | tf_op jit(solution)/shard_map/pack/pallas_call | solution.py:307
  2.1 11.2 %all-to-all-start = ((bf16[32,56,128]{2,1,0:T(8,128)(2,1)}), bf16[32,56,128]{2,1,0:T(8,128)(2,1)}, u32[]{:S(2)}, u32[]{:S(2)}) async-start(bf16[32,56,128]{2,1,0:T(8,128)(2,1)} %pack.1), calls=%async_computation | async-start | bytes 917504 | tf_op jit(solution)/shard_map/all_to_all | solution.py:282
  13.4 0.7 broadcast_in_dim.7.spec_weight_ref
  14.0 0.0 copy-done.2
  14.1 0.0 copy-start.3
  14.1 0.4 reshape_squeeze.3
  14.4 0.0 copy-start.4
  14.4 0.1 copy.10
  14.5 0.0 copy-start
  14.6 0.9 true_power.1
  15.5 0.1 collective-permute-start
  15.6 0.0 copy-done.3
  15.6 0.1 fusion.3
  15.7 0.1 fusion.2
  15.8 0.0 copy-done.4
  15.8 0.1 fusion.1
  15.9 0.1 pad_add_fusion.1
  16.0 0.1 reshape.9
  16.1 0.1 fusion
  16.2 0.1 pad_maximum_fusion.1
  16.2 0.1 reshape.10
  16.3 0.4 collective-permute-done
  16.8 3.0 %collective-permute-start.3 = (f32[8,128]{1,0:T(8,128)S(1)}, f32[8,128]{1,0:T(8,128)S(1)}, u32[]{:S(2)}, u32[]{:S(2)}) collective-permute-start(f32[8,128]{1,0:T(8,128)S(1)} %add.18.refs_0_), channel_id=1, source_target_pairs={{0,6},{1,7},{2,0},{3,1},{4,2},{5,3},{6,4},{7,5},{8,14},{9,15},{10,... | collective-permute-start | bytes 12296 | tf_op jit(solution)/shard_map/ppermute | solution.py:289
  19.8 0.6 collective-permute-start.2
  20.4 1.0 collective-permute-start.1
  21.4 0.0 collective-permute-done.3.refs_3_
  21.4 3.5 %collective-permute-done.2.refs_2_ = f32[8,128]{1,0:T(8,128)S(1)} collective-permute-done((f32[8,128]{1,0:T(8,128)S(1)}, f32[8,128]{1,0:T(8,128)S(1)}, u32[]{:S(2)}, u32[]{:S(2)}) %collective-permute-start.2) | collective-permute-done | bytes 4128 | tf_op jit(solution)/shard_map/ppermute | solution.py:289
  24.9 0.3 collective-permute-done.1.refs_1_
  25.3 4.3 %all-to-all-done.buf_ref = bf16[32,56,128]{2,1,0:T(8,128)(2,1)} async-done(((bf16[32,56,128]{2,1,0:T(8,128)(2,1)}), bf16[32,56,128]{2,1,0:T(8,128)(2,1)}, u32[]{:S(2)}, u32[]{:S(2)}) %all-to-all-start) | async-done | bytes 458784 | tf_op jit(solution)/shard_map/all_to_all | solution.py:282
  29.6 0.0 copy-done
  29.6 20.9 %forward.1 = (bf16[256,1280]{1,0:T(8,128)(2,1)S(1)}, f32[32,1,2048]{2,1,0:T(1,128)S(1)}) custom-call(f32[8]{0:T(128)S(1)} %add_cosine_fusion.lat_ref, bf16[32,56,128]{2,1,0:T(8,128)(2,1)} %all-to-all-done.buf_ref, s32[3,9,1280]{2,1,0:T(8,128)S(1)} %pad_add_fusion.cell_ref, f32[3,9,1280]{2,1,0:T(8,128)S(1)} %pad_maximum_fusion.weight_ref, ...), custom_call_target="tpu_custom_call" | custom-call | tf_op jit(solution)/shard_map/forward/pallas_call | solution.py:341
  50.5 16.6 %all_to_all.20.parts_ref = f32[32,1,2048]{2,1,0:T(1,128)S(1)} all-to-all(f32[32,1,2048]{2,1,0:T(1,128)S(1)} %get-tuple-element.22), channel_id=1, replica_groups=mesh['band'=32,'chan'=8] {'band'}, dimensions={0} | all-to-all | bytes 524288 | tf_op jit(solution)/shard_map/all_to_all | solution.py:282
  67.1 0.2 middle.1
  67.3 14.4 %all_to_all.21.factor_ref = f32[32,1,1280]{2,1,0:T(1,128)S(1)} all-to-all(f32[32,1,1280]{2,1,0:T(1,128)S(1)} %middle.1), channel_id=1, replica_groups=mesh['band'=32,'chan'=8] {'band'}, dimensions={0} | all-to-all | bytes 327680 | tf_op jit(solution)/shard_map/all_to_all | solution.py:282
  81.7 0.0 copy-start.1
  81.7 18.7 %backward.1 = bf16[32,56,128]{2,1,0:T(8,128)(2,1)S(1)} custom-call(f32[8]{0:T(128)S(1)} %add_cosine_fusion.lat_ref, s32[3,9,1280]{2,1,0:T(8,128)S(1)} %pad_add_fusion.cell_ref, f32[3,9,1280]{2,1,0:T(8,128)S(1)} %pad_maximum_fusion.weight_ref, bf16[1280,768]{1,0:T(8,128)(2,1)S(1)} %copy-done, bf16[256,1280]{1,0:T(8,128)(2,1)S(1)} %bitcast.8, ...), custom_call_target="tpu_custom_call" | custom-call | tf_op jit(solution)/shard_map/backward/pallas_call | solution.py:370
  100.4 17.9 %all_to_all.22.blocks_ref = bf16[32,56,128]{2,1,0:T(8,128)(2,1)S(1)} all-to-all(bf16[32,56,128]{2,1,0:T(8,128)(2,1)S(1)} %backward.1), channel_id=1, replica_groups=mesh['band'=32,'chan'=8] {'band'}, dimensions={0} | all-to-all | bytes 917504 | tf_op jit(solution)/shard_map/all_to_all | solution.py:282
  118.3 0.0 copy-done.1
  118.3 1.3 %unpack.1 = bf16[28,4096]{1,0:T(8,128)(2,1)} custom-call(s32[32]{0:T(128)S(1)} %copy-done.1, bf16[32,56,128]{2,1,0:T(8,128)(2,1)S(1)} %all_to_all.22.blocks_ref), custom_call_target="tpu_custom_call" | custom-call | tf_op jit(solution)/shard_map/unpack/pallas_call | solution.py:385
  (5 shorter events, 0.1 us)
Async XLA Ops:
  0.0 14.0 %copy-start.2 = (bf16[1,28,8,2,640]{4,3,2,1,0:T(2,128)(2,1)S(1)}, bf16[1,28,8,2,640]{4,3,2,1,0:T(2,128)(2,1)}, u32[]{:S(2)}) copy-start(bf16[1,28,8,2,640]{4,3,2,1,0:T(2,128)(2,1)} %param.11) | copy-start | bytes 1720324
  2.1 27.5 %all-to-all-start = ((bf16[32,56,128]{2,1,0:T(8,128)(2,1)}), bf16[32,56,128]{2,1,0:T(8,128)(2,1)}, u32[]{:S(2)}, u32[]{:S(2)}) async-start(bf16[32,56,128]{2,1,0:T(8,128)(2,1)} %pack.1), calls=%async_computation | async-start | bytes 917504 | tf_op jit(solution)/shard_map/all_to_all | solution.py:282
  14.1 1.6 %copy-start.3 = (s32[3,8,1440]{2,1,0:T(8,128)S(1)}, s32[3,8,1440]{2,1,0:T(8,128)}, u32[]{:S(2)}) copy-start(s32[3,8,1440]{2,1,0:T(8,128)} %param.9) | copy-start | bytes 414724
  14.4 1.4 %copy-start.4 = (f32[3,8,1440]{2,1,0:T(8,128)S(1)}, f32[3,8,1440]{2,1,0:T(8,128)}, u32[]{:S(2)}) copy-start(f32[3,8,1440]{2,1,0:T(8,128)} %param.10) | copy-start | bytes 414724
  14.5 15.0 %copy-start = (bf16[1280,768]{1,0:T(8,128)(2,1)S(1)}, bf16[1280,768]{1,0:T(8,128)(2,1)}, u32[]{:S(2)}) copy-start(bf16[1280,768]{1,0:T(8,128)(2,1)} %constant.20.clone.table_ref) | copy-start | bytes 5898244
  15.5 1.3 %collective-permute-start = (f32[8,128]{1,0:T(8,128)S(1)}, f32[8,128]{1,0:T(8,128)S(1)}, u32[]{:S(2)}, u32[]{:S(2)}) collective-permute-start(f32[8,128]{1,0:T(8,128)S(1)} %get-tuple-element.20), channel_id=1, source_target_pairs={{0,1},{1,0},{2,3},{3,2},{4,5},{5,4},{6,7},{7,6},{8,9},{9,8},{10,11... | collective-permute-start | bytes 12296 | tf_op jit(solution)/shard_map/ppermute | solution.py:287
  16.8 4.6 %collective-permute-start.3 = (f32[8,128]{1,0:T(8,128)S(1)}, f32[8,128]{1,0:T(8,128)S(1)}, u32[]{:S(2)}, u32[]{:S(2)}) collective-permute-start(f32[8,128]{1,0:T(8,128)S(1)} %add.18.refs_0_), channel_id=1, source_target_pairs={{0,6},{1,7},{2,0},{3,1},{4,2},{5,3},{6,4},{7,5},{8,14},{9,15},{10,... | collective-permute-start | bytes 12296 | tf_op jit(solution)/shard_map/ppermute | solution.py:289
  19.8 5.1 %collective-permute-start.2 = (f32[8,128]{1,0:T(8,128)S(1)}, f32[8,128]{1,0:T(8,128)S(1)}, u32[]{:S(2)}, u32[]{:S(2)}) collective-permute-start(f32[8,128]{1,0:T(8,128)S(1)} %add.18.refs_0_), channel_id=1, source_target_pairs={{0,4},{1,5},{2,6},{3,7},{4,0},{5,1},{6,2},{7,3},{8,12},{9,13},{10,... | collective-permute-start | bytes 12296 | tf_op jit(solution)/shard_map/ppermute | solution.py:289
  20.4 4.8 %collective-permute-start.1 = (f32[8,128]{1,0:T(8,128)S(1)}, f32[8,128]{1,0:T(8,128)S(1)}, u32[]{:S(2)}, u32[]{:S(2)}) collective-permute-start(f32[8,128]{1,0:T(8,128)S(1)} %add.18.refs_0_), channel_id=1, source_target_pairs={{0,2},{1,3},{2,4},{3,5},{4,6},{5,7},{6,0},{7,1},{8,10},{9,11},{10,... | collective-permute-start | bytes 12296 | tf_op jit(solution)/shard_map/ppermute | solution.py:289
  81.7 36.6 %copy-start.1 = (s32[32]{0:T(128)S(1)}, s32[32]{0:T(128)}, u32[]{:S(2)}) copy-start(s32[32]{0:T(128)} %slot_ref.3) | copy-start | bytes 388
